TPU v7x, 256 devices: a whole 4x4x8 slice. The times are simulated.
256 devices in a mesh: row: 16 (over z, core), col: 16 (over y, x).
Axes of the slice: x: 4, y: 4, z: 8, core: 2. Of those that a mesh axis runs over, the one named last changes fastest.
Arguments:
- hamiltonian: float32 [8, 16, 128, 8, 16, 128], P(None, 'row', None, None, 'col'), may hold values from -4 to 4, as said below
Outputs:
- band_form: float32 [8, 16, 128, 8, 16, 128], P(None, 'row', None, None, 'col')
Inputs may be any that keep to these rules, and one draw needn't show every extreme that they name: The matrix laid out by hamiltonian is symmetric.
All inputs are finite; a program needn't handle non-finite values.
Results may differ from a plain program's by a relative error of at most 0.0001.
Values sent between devices are 32-bit elements; how exact they have to be, the bound alone decides.
A program may use at most 64 MiB of HBM per device.

v0:
```python
import jax
import jax.numpy as jnp
from jax import lax
from jax.sharding import PartitionSpec as P

PANELS = 2


def broadcast(array, axis, root):
    mine = lax.axis_index(axis) == root
    return lax.psum(jnp.where(mine, array, jnp.zeros_like(array)), axis)


def product(first, second):
    return jnp.dot(first, second, precision=lax.Precision.HIGHEST)


def decompose(square):
    count = square.shape[0]
    positions = jnp.arange(count)

    def sweep(column_index, work):
        pivot_row = work[column_index]
        column = work[:, column_index] / pivot_row[column_index]
        below = jnp.where(positions > column_index, column, 0.0)
        after = jnp.where(positions > column_index, pivot_row, 0.0)
        work = work - below[:, None] * after[None, :]
        return work.at[:, column_index].set(
            jnp.where(positions > column_index, below, work[:, column_index])
        )

    work = lax.fori_loop(0, count, sweep, square)
    unit_lower = jnp.tril(work, -1) + jnp.eye(count, dtype=work.dtype)
    return (unit_lower, jnp.triu(work))


def factor_panel(gram_sum, top_block):
    lower_factor = jnp.linalg.cholesky(gram_sum)
    top_q = jax.scipy.linalg.solve_triangular(lower_factor, top_block.T, lower=True).T
    unit_lower, upper_part = decompose(top_q + jnp.eye(top_q.shape[0], dtype=top_q.dtype))
    coupling = jax.scipy.linalg.solve_triangular(
        unit_lower, upper_part.T, lower=True, unit_diagonal=True
    ).T
    return (lower_factor, unit_lower, upper_part, coupling)


def to_columns(values, row_tiles, tile_width):
    row_count = lax.axis_size("row")
    col_count = lax.axis_size("col")
    row_index = lax.axis_index("row")
    col_index = lax.axis_index("col")
    row_ratio = row_count // col_count
    tiled = values.reshape(row_tiles, tile_width, values.shape[1])
    slot_ids = jnp.arange(row_ratio)
    chosen = (slot_ids == (row_index - col_index) // col_count) & (
        (row_index - col_index) % col_count == 0
    )
    placed = jnp.where(chosen[None, :, None, None], tiled[:, None], 0.0)
    gathered = lax.psum(placed, "row")
    return gathered.reshape(-1, values.shape[1])


def write_band(local_block, band_block, number, row_tile, col_tile):
    row_tiles = row_tile.shape[0]
    col_tiles = col_tile.shape[0]
    tile_width = band_block.shape[0]
    blocks = local_block.reshape(row_tiles, tile_width, col_tiles, tile_width)
    row_grid = row_tile[:, None, None, None]
    col_grid = col_tile[None, None, :, None]
    blocks = jnp.where(
        (row_grid == number + 1) & (col_grid == number), band_block[None, :, None, :], blocks
    )
    blocks = jnp.where((row_grid > number + 1) & (col_grid == number), 0.0, blocks)
    blocks = jnp.where(
        (row_grid == number) & (col_grid == number + 1), band_block.T[None, :, None, :], blocks
    )
    blocks = jnp.where((row_grid == number) & (col_grid > number + 1), 0.0, blocks)
    return blocks.reshape(local_block.shape)


def local(hamiltonian):
    row_tiles = hamiltonian.shape[0]
    tile_width = hamiltonian.shape[2]
    col_tiles = hamiltonian.shape[3]
    row_count = lax.axis_size("row")
    col_count = lax.axis_size("col")
    row_index = lax.axis_index("row")
    col_index = lax.axis_index("col")
    local_block = hamiltonian.reshape(row_tiles * tile_width, col_tiles * tile_width)
    row_tile = jnp.arange(row_tiles) * row_count + row_index
    col_tile = jnp.arange(col_tiles) * col_count + col_index
    row_tile_of = jnp.repeat(row_tile, tile_width)
    pending = None
    for number in range(PANELS):
        owned_slot = number // col_count
        owned = local_block[:, owned_slot * tile_width : (owned_slot + 1) * tile_width]
        panel_rows = broadcast(owned, "col", number % col_count)
        panel_rows = jnp.where((row_tile_of > number)[:, None], panel_rows, 0.0)
        top_slot = (number + 1) // row_count
        top_part = jnp.where(
            row_index == (number + 1) % row_count,
            panel_rows[top_slot * tile_width : (top_slot + 1) * tile_width],
            0.0,
        )
        gram_sum, top_block = lax.psum((product(panel_rows.T, panel_rows), top_part), "row")
        lower_factor, unit_lower, upper_part, coupling = factor_panel(gram_sum, top_block)
        lower_q = jax.scipy.linalg.solve_triangular(lower_factor, panel_rows.T, lower=True)
        lower_y = jax.scipy.linalg.solve_triangular(upper_part.T, lower_q, lower=True).T
        tiled = lower_y.reshape(row_tiles, tile_width, tile_width)
        tiled = jnp.where(
            (row_tile == number + 1)[:, None, None],
            unit_lower[None],
            jnp.where((row_tile > number + 1)[:, None, None], tiled, 0.0),
        )
        vectors = tiled.reshape(-1, tile_width)
        col_vectors = to_columns(vectors, row_tiles, tile_width)
        products = lax.psum(product(local_block, col_vectors), "col")
        products = jnp.where((row_tile_of > number)[:, None], products, 0.0)
        applied = product(products, coupling)
        inner_sums = lax.psum(product(vectors.T, applied), "row")
        correction = applied - 0.5 * product(vectors, product(coupling.T, inner_sums))
        col_correct = to_columns(correction, row_tiles, tile_width)
        left_side = jnp.concatenate([correction, vectors], 1)
        right_side = jnp.concatenate([col_vectors, col_correct], 1)
        local_block = local_block - product(left_side, right_side.T)
        local_block = write_band(local_block, -lower_factor.T, number, row_tile, col_tile)
    return local_block.reshape(hamiltonian.shape)


def solution(mesh):
    in_specs = (P(None, "row", None, None, "col", None),)
    out_specs = P(None, "row", None, None, "col", None)
    return jax.shard_map(local, mesh=mesh, in_specs=in_specs, out_specs=out_specs, check_vma=False)
```

profile of v0, /device:TPU:1, one launch (start us, length us, event | category | flops | bytes accessed | tf_op | source)
XLA Modules:
  0.0 2319.3 jit_solution(13821584353645791140)
XLA Ops:
  14.0 97.6 %all-reduce.15.cloned.1.call-done = f32[1024,128]{1,0:T(8,128)} async-done(((f32[1024,128]{1,0:T(8,128)}), f32[1024,128]{1,0:T(8,128)}) %all-reduce.15.cloned.1.call-update) | async-done | bytes 524304 | tf_op jit(solution)/shard_map/psum | solution.py:11
  115.4 108.4 %all-reduce.37.cloned.1.call-done = (f32[128,128]{0,1:T(8,128)}, f32[128,128]{0,1:T(8,128)}) async-done(((f32[128,128]{0,1:T(8,128)}, f32[128,128]{0,1:T(8,128)}), (f32[128,128]{0,1:T(8,128)}, f32[128,128]{0,1:T(8,128)})) %all-reduce.37.cloned.1.call-update) | async-done | bytes 131088 | tf_op jit(solution)/shard_map/psum | solution.py:105
  225.6 11.7 cholesky.44
  238.6 9.8 custom-call.16
  250.2 443.8 %while.36 = (s32[]{:T(128)}, f32[128,128]{0,1:T(8,128)S(1)}, s32[]{:T(128)}, s32[]{:T(128)}, s32[]{:T(128)}, /*index=5*/s32[1]{0:T(128)}) while((s32[]{:T(128)}, f32[128,128]{0,1:T(8,128)S(1)}, s32[]{:T(128)}, s32[]{:T(128)}, s32[]{:T(128)}, /*index=5*/s32[1]{0:T(128)}) %tuple.119), condition=%wide.region_7.10_spmd.clone, body=%wide.region_5.9_spmd.clone.sunk | while | flops 34062 | bytes 403574 | solution.py:32
  694.4 9.8 custom-call.18
  706.6 109.6 %all-reduce.17.cloned.1.call-done = f32[1024,128]{1,0:T(8,128)} async-done(((f32[1024,128]{1,0:T(8,128)}), f32[1024,128]{1,0:T(8,128)}) %all-reduce.17.cloned.1.call-update) | async-done | bytes 524304 | tf_op jit(solution)/shard_map/psum | solution.py:59
  823.0 9.8 custom-call.19
  833.1 84.2 %all-reduce.19.cloned.1.call-done = f32[1024,128]{1,0:T(8,128)} async-done(((f32[1024,128]{1,0:T(8,128)}), f32[1024,128]{1,0:T(8,128)}) %all-reduce.19.cloned.1.call-update) | async-done | bytes 524304 | tf_op jit(solution)/shard_map/psum | solution.py:117
  921.0 99.9 %all-reduce.21.cloned.1.call-done = f32[128,128]{1,0:T(8,128)} async-done(((f32[128,128]{1,0:T(8,128)}), f32[128,128]{1,0:T(8,128)}) %all-reduce.21.cloned.1.call-update) | async-done | bytes 65552 | tf_op jit(solution)/shard_map/psum | solution.py:120
  1024.0 107.3 %all-reduce.23.cloned.1.call-done = f32[1024,128]{1,0:T(8,128)} async-done(((f32[1024,128]{1,0:T(8,128)}), f32[1024,128]{1,0:T(8,128)}) %all-reduce.23.cloned.1.call-update) | async-done | bytes 524304 | tf_op jit(solution)/shard_map/psum | solution.py:59
  1134.0 6.7 fusion.8
  1143.7 94.3 %all-reduce.25.cloned.1.call-done = f32[1024,128]{1,0:T(8,128)} async-done(((f32[1024,128]{1,0:T(8,128)}), f32[1024,128]{1,0:T(8,128)}) %all-reduce.25.cloned.1.call-update) | async-done | bytes 524304 | tf_op jit(solution)/shard_map/psum | solution.py:11
  1241.9 108.4 %all-reduce.35.cloned.1.call-done = (f32[128,128]{0,1:T(8,128)}, f32[128,128]{0,1:T(8,128)}) async-done(((f32[128,128]{0,1:T(8,128)}, f32[128,128]{0,1:T(8,128)}), (f32[128,128]{0,1:T(8,128)}, f32[128,128]{0,1:T(8,128)})) %all-reduce.35.cloned.1.call-update) | async-done | bytes 131088 | tf_op jit(solution)/shard_map/psum | solution.py:105
  1352.0 11.7 cholesky.55
  1365.1 9.8 custom-call.20
  1376.7 475.2 %while.37 = (s32[]{:T(128)}, f32[128,128]{0,1:T(8,128)S(1)}, s32[]{:T(128)}, s32[]{:T(128)}, s32[]{:T(128)}, /*index=5*/s32[1]{0:T(128)}) while((s32[]{:T(128)}, f32[128,128]{0,1:T(8,128)S(1)}, s32[]{:T(128)}, s32[]{:T(128)}, s32[]{:T(128)}, /*index=5*/s32[1]{0:T(128)}) %tuple.122), condition=%wide.region_17.22_spmd.clone, body=%wide.region_15.21_spmd.clone.sunk | while | flops 34062 | bytes 403574 | solution.py:32
  1852.3 9.8 custom-call.22
  1864.5 109.7 %all-reduce.27.cloned.1.call-done = f32[1024,128]{1,0:T(8,128)} async-done(((f32[1024,128]{1,0:T(8,128)}), f32[1024,128]{1,0:T(8,128)}) %all-reduce.27.cloned.1.call-update) | async-done | bytes 524304 | tf_op jit(solution)/shard_map/psum | solution.py:59
  1980.8 9.8 custom-call.23
  1990.9 84.4 %all-reduce.29.cloned.1.call-done = f32[1024,128]{1,0:T(8,128)} async-done(((f32[1024,128]{1,0:T(8,128)}), f32[1024,128]{1,0:T(8,128)}) %all-reduce.29.cloned.1.call-update) | async-done | bytes 524304 | tf_op jit(solution)/shard_map/psum | solution.py:117
  2079.0 99.9 %all-reduce.31.cloned.1.call-done = f32[128,128]{1,0:T(8,128)} async-done(((f32[128,128]{1,0:T(8,128)}), f32[128,128]{1,0:T(8,128)}) %all-reduce.31.cloned.1.call-update) | async-done | bytes 65552 | tf_op jit(solution)/shard_map/psum | solution.py:120
  2181.4 107.8 %all-reduce.33.cloned.1.call-done = f32[1024,128]{1,0:T(8,128)} async-done(((f32[1024,128]{1,0:T(8,128)}), f32[1024,128]{1,0:T(8,128)}) %all-reduce.33.cloned.1.call-update) | async-done | bytes 524304 | tf_op jit(solution)/shard_map/psum | solution.py:59
  2298.0 14.3 broadcast_select_fusion.5
  (2414 shorter events, 973.6 us)
Async XLA Ops:
  6.5 105.1 %all-reduce.15.cloned.1.call-start = ((), (), s32[]{:S(2)}) async-start(), calls=%async_computation | async-start | bytes 1048576 | tf_op jit(solution)/shard_map/psum | solution.py:11
  13.6 210.1 %all-reduce.37.cloned.1.call-start = ((), (), s32[]{:S(2)}) async-start(), calls=%async_computation.11 | async-start | bytes 262144 | tf_op jit(solution)/shard_map/psum | solution.py:105
  115.1 701.1 %all-reduce.17.cloned.1.call-start = ((), (), s32[]{:S(2)}) async-start(), calls=%async_computation.1 | async-start | bytes 1048576 | tf_op jit(solution)/shard_map/psum | solution.py:59
  706.3 211.0 %all-reduce.19.cloned.1.call-start = ((), (), s32[]{:S(2)}) async-start(), calls=%async_computation.2 | async-start | bytes 1048576 | tf_op jit(solution)/shard_map/psum | solution.py:117
  822.8 198.1 %all-reduce.21.cloned.1.call-start = ((), (), s32[]{:S(2)}) async-start(), calls=%async_computation.3 | async-start | bytes 131072 | tf_op jit(solution)/shard_map/psum | solution.py:120
  920.7 210.5 %all-reduce.23.cloned.1.call-start = ((), (), s32[]{:S(2)}) async-start(), calls=%async_computation.4 | async-start | bytes 1048576 | tf_op jit(solution)/shard_map/psum | solution.py:59
  1023.3 214.7 %all-reduce.25.cloned.1.call-start = ((), (), s32[]{:S(2)}) async-start(), calls=%async_computation.5 | async-start | bytes 1048576 | tf_op jit(solution)/shard_map/psum | solution.py:11
  1131.5 2.2 copy-start.1
  1131.5 2.3 copy-start.3
  1131.5 2.4 copy-start.4
  1140.7 2.0 copy-start
  1143.6 206.7 %all-reduce.35.cloned.1.call-start = ((), (), s32[]{:S(2)}) async-start(), calls=%async_computation.10 | async-start | bytes 262144 | tf_op jit(solution)/shard_map/psum | solution.py:105
  1241.6 732.6 %all-reduce.27.cloned.1.call-start = ((), (), s32[]{:S(2)}) async-start(), calls=%async_computation.6 | async-start | bytes 1048576 | tf_op jit(solution)/shard_map/psum | solution.py:59
  1864.3 211.0 %all-reduce.29.cloned.1.call-start = ((), (), s32[]{:S(2)}) async-start(), calls=%async_computation.7 | async-start | bytes 1048576 | tf_op jit(solution)/shard_map/psum | solution.py:117
  1980.7 308.5 %copy-start.2 = (f32[1024,128]{1,0:T(8,128)S(1)}, f32[1024,128]{1,0:T(8,128)}, u32[]{:S(2)}) copy-start(f32[1024,128]{1,0:T(8,128)} %all-reduce.27.cloned.1.call-done) | copy-start | bytes 1572868
  1980.7 198.1 %all-reduce.31.cloned.1.call-start = ((), (), s32[]{:S(2)}) async-start(), calls=%async_computation.8 | async-start | bytes 131072 | tf_op jit(solution)/shard_map/psum | solution.py:120
  2078.7 210.5 %all-reduce.33.cloned.1.call-start = ((), (), s32[]{:S(2)}) async-start(), calls=%async_computation.9 | async-start | bytes 1048576 | tf_op jit(solution)/shard_map/psum | solution.py:59
Sparse Core Ops, SparseCore 0:
  13.8 97.7 all-reduce.14
  115.2 108.4 all-reduce.36
  706.4 109.7 all-reduce.16
  822.9 94.3 all-reduce.18
  920.9 99.9 all-reduce.20
  1023.5 107.7 all-reduce.22
  1143.7 94.2 all-reduce.24
  1241.7 108.5 all-reduce.34
  1864.4 109.7 all-reduce.26
  1980.9 94.3 all-reduce.28
  2078.8 99.9 all-reduce.30
  2181.4 107.7 all-reduce.32
where the time goes:
time: 2350 us; the launch traced here: 2320 us
  waiting for transfers between devices  1210 us (51%)
  other arithmetic  820 us (35%)
  local copies, waits for them, and re-layouts  209 us (9%)
  matrix products  46.7 us (2%)
    another operation x512, other arithmetic  525 us
    psum x4, waiting for transfers between devices, to_columns(): gathered = lax.psum(placed, 'row')  434 us
    psum x2, waiting for transfers between devices, local(): lax.psum((product(panel_rows.T, panel_rows), top_part), 'row')  217 us
    psum x2, waiting for transfers between devices, local(): inner_sums = lax.psum(product(vectors.T, applied), 'row')  200 us
    psum x2, waiting for transfers between devices, broadcast(): return lax.psum(jnp.where(mine, array, jnp.zeros_like(array)), axis)  192 us
    psum x2, waiting for transfers between devices, local(): products = lax.psum(product(local_block, col_vectors), 'col')  169 us
    mul x512, other arithmetic, sweep(): work = work - below[:, None] * after[None, :]  164 us
    dynamic_slice x256, local copies, waits for them, and re-layouts, sweep(): column = work[:, column_index] / pivot_row[column_index]  159 us
  transfers between devices with their start and end apart: 12, of which 12 were waited for; matrix products, arithmetic and copies ran while one was open for 1% of the time, Pallas kernels for 0%

commit v1 on v0

v1 whole, which is shorter than its diff:
```python
import functools

import jax
import jax.numpy as jnp
from jax import lax
from jax.experimental import pallas as pl
from jax.experimental.pallas import tpu as pltpu
from jax.sharding import PartitionSpec as P

MESH = pl.DeviceIdType.MESH
NB = 128
NN = (((1,), (0,)), ((), ()))
NT = (((1,), (1,)), ((), ()))
TN = (((0,), (0,)), ((), ()))
VMEM_LIMIT = 56 << 20


def split(value):
    high = value.astype(jnp.bfloat16)
    low = (value - high.astype(jnp.float32)).astype(jnp.bfloat16)
    return high, low


def mxu(first, second, dims):
    return lax.dot_general(first, second, dims, preferred_element_type=jnp.float32)


def dot3(first, second, dims):
    fh, fl = split(first)
    sh, sl = split(second)
    return mxu(fh, sh, dims) + (mxu(fh, sl, dims) + mxu(fl, sh, dims))


def exact(first, second, dims=NN):
    return lax.dot_general(
        first, second, dims, precision=lax.Precision.HIGHEST, preferred_element_type=jnp.float32
    )


def iota(axis, shape):
    return lax.broadcasted_iota(jnp.int32, shape, axis)


def cholesky_blocks(g_ref, r_ref, first, last):
    sub = iota(0, (8, NB))
    lane = iota(1, (8, NB))

    def block(k, carry):
        base = pl.multiple_of(k * 8, 8)
        x = g_ref[pl.ds(base, 8), :]
        rolled = pltpu.roll(x, lax.rem(NB - base, NB), 1)
        cols = [jnp.broadcast_to(rolled[:, i : i + 1], (8, NB)) for i in range(8)]
        for i in range(8):
            scale = lax.rsqrt(cols[i][i : i + 1, :])
            column = cols[i] * scale
            below = jnp.where(sub > i, column, 0.0)
            row = x[i : i + 1, :] * scale
            x = jnp.where(sub == i, row, x - below * row)
            for m in range(i + 1, 8):
                cols[m] = cols[m] - below * column[m : m + 1, :]
        x = jnp.where(lane >= base + sub, x, 0.0)
        r_ref[pl.ds(base, 8), :] = x
        g_ref[...] -= exact(x, x, TN)
        return carry

    lax.fori_loop(first, last, block, 0)


def inverse_blocks(y_ref, t_ref, first, last):
    sub = iota(0, (8, NB))
    lane = iota(1, (8, NB))
    wide = iota(1, (NB, NB))

    def block(k, carry):
        base = pl.multiple_of(k * 8, 8)
        x = y_ref[pl.ds(base, 8), :]
        rolled = pltpu.roll(x, lax.rem(NB - base, NB), 1)
        cols = [jnp.broadcast_to(rolled[:, i : i + 1], (8, NB)) for i in range(8)]
        inside = (lane >= base) & (lane < base + 8)
        x = jnp.where(inside, jnp.where(lane - base == sub, 1.0, 0.0), x)
        for i in range(8):
            scale = 1.0 / cols[i][i : i + 1, :]
            factor = jnp.where(sub == i, 0.0, cols[i])
            row = x[i : i + 1, :] * scale
            x = jnp.where(sub == i, row, x - factor * row)
            for m in range(i + 1, 8):
                entry = cols[m][i : i + 1, :] * scale
                cols[m] = jnp.where(sub == i, entry, cols[m] - factor * entry)
        t_ref[pl.ds(base, 8), :] = x
        y = y_ref[...]
        chosen = (wide >= base) & (wide < base + 8)
        y_ref[...] = jnp.where(chosen, 0.0, y) - exact(jnp.where(chosen, y, 0.0), t_ref[...])
        y_ref[pl.ds(base, 8), :] = x
        t_ref[pl.ds(base, 8), :] = jnp.zeros((8, NB), jnp.float32)
        return carry

    lax.fori_loop(first, last, block, 0)


def reduce_kernel(n, tiles, *refs):
    rows = tiles * NB
    ch = rows // n
    pc = NB // n
    half = n // 2
    (
        a_hbm,
        c0r, f0r, c1r, f1r, c0c, f0c, c1c, f1c, r0_ref, r1_ref,
        abuf, ahi, alo, stg_r, stg_c, xr, xc, wpart, wrs, wch, wr, wc,
        ar_src, ar_slot, ar_res, h_src, h_slot, h_piece, h_ex, h_res,
        g_ref, y_ref, t_ref, asem, ss, rs,
    ) = refs
    r = lax.axis_index("row")
    c = lax.axis_index("col")
    parity = lax.rem(r, 2)
    level = r // 2

    load = pltpu.make_async_copy(a_hbm, abuf, asem)
    load.start()
    barrier = pltpu.get_barrier_semaphore()

    def greet(k, carry):
        pl.semaphore_signal(barrier, inc=1, device_id=(lax.rem(r + k, n), c), device_id_type=MESH)
        pl.semaphore_signal(barrier, inc=1, device_id=(r, lax.rem(c + k, n)), device_id_type=MESH)
        return carry

    lax.fori_loop(1, n, greet, 0)

    @pl.when(r != c)
    def _():
        pl.semaphore_signal(barrier, inc=1, device_id=(c, r), device_id_type=MESH)

    pl.semaphore_wait(barrier, 2 * (n - 1) + jnp.where(r != c, 1, 0))

    def send(src, dst, sem, device):
        pltpu.make_async_remote_copy(
            src, dst, ss.at[sem], rs.at[sem], device_id=device, device_id_type=MESH
        ).start()

    def over_cols(sem, src_of, dst_of):
        def one(k, carry):
            j = lax.rem(c + k, n)
            send(src_of(j), dst_of(j), sem, (r, j))
            return carry

        lax.fori_loop(1, n, one, 0)

    def over_rows(sem, src_of, dst_of):
        def one(k, carry):
            j = lax.rem(r + k, n)
            send(src_of(j), dst_of(j), sem, (j, c))
            return carry

        lax.fori_loop(1, n, one, 0)

    def wait(sem, sent, received):
        pltpu.make_async_copy(received, received, rs.at[sem]).wait()
        pltpu.make_async_copy(sent, sent, ss.at[sem]).wait()

    def scatter(t):
        @pl.when(c == t)
        def _():
            over_cols(
                t,
                lambda j: stg_r.at[pl.ds(j * ch, ch)],
                lambda j: xr.at[t, pl.ds(j * ch, ch)],
            )
            xr[t, pl.ds(t * ch, ch), :] = stg_r[pl.ds(t * ch, ch), :]

        @pl.when(r == t)
        def _():
            over_rows(
                3 + t,
                lambda j: stg_c.at[pl.ds(j * ch, ch)],
                lambda j: xc.at[t, j // 2, lax.rem(j, 2)],
            )
            xc[t, t // 2, t % 2] = stg_c[pl.ds(t * ch, ch), :]

    def scatter_wait(t):
        @pl.when(c == t)
        def _():
            sent = stg_r.at[pl.ds(0, (n - 1) * ch)]
            pltpu.make_async_copy(sent, sent, ss.at[t]).wait()

        @pl.when(c != t)
        def _():
            got = xr.at[t, pl.ds(c * ch, ch)]
            pltpu.make_async_copy(got, got, rs.at[t]).wait()

        @pl.when(r == t)
        def _():
            sent = stg_c.at[pl.ds(0, (n - 1) * ch)]
            pltpu.make_async_copy(sent, sent, ss.at[3 + t]).wait()

        @pl.when(r != t)
        def _():
            got = xc.at[t, level, parity]
            pltpu.make_async_copy(got, got, rs.at[3 + t]).wait()

    def gather_cols_start(buf, sem):
        mine = buf.at[pl.ds(c * ch, ch)]
        over_cols(sem, lambda j: mine, lambda j: mine)

    def gather_cols_wait(buf, sem):
        part = buf.at[pl.ds(0, (n - 1) * ch)]
        wait(sem, part, part)

    def gather_rows_start(buf, sem):
        mine = buf.at[level, parity]

        def one(k, carry):
            send(mine, mine, sem, (lax.rem(level + k, half) * 2 + parity, c))
            return carry

        lax.fori_loop(1, half, one, 0)

    def gather_rows_mid(buf, sem):
        part = buf.at[pl.ds(0, half - 1), 0]
        wait(sem, part, part)
        mine = buf.at[:, parity]
        send(mine, mine, sem + 1, (r + 1 - 2 * parity, c))

    def gather_rows_wait(buf, sem):
        part = buf.at[:, 0]
        wait(sem + 1, part, part)

    def sum_start(q, parts, sem):
        count = len(parts)
        for i, part in enumerate(parts):
            ar_src[q, i] = part
        over_cols(
            sem,
            lambda j: ar_src.at[q, pl.ds(0, count), pl.ds(j * pc, pc)],
            lambda j: ar_slot.at[q, c, pl.ds(0, count)],
        )
        ar_slot[q, c, 0:count] = ar_src[q, 0:count, pl.ds(c * pc, pc), :]

    def sum_mid(q, count, sem):
        got = ar_slot.at[q, pl.ds(0, n - 1), pl.ds(0, count)]
        wait(sem, got, got)
        total = ar_slot[q, 0, 0:count]
        for j in range(1, n):
            total = total + ar_slot[q, j, 0:count]
        mine = (q, pl.ds(0, count), pl.ds(c * pc, pc))
        ar_res[q, 0:count, pl.ds(c * pc, pc), :] = total
        over_cols(sem + 1, lambda j: ar_res.at[mine], lambda j: ar_res.at[mine])

    def sum_wait(q, count, sem):
        got = ar_res.at[q, pl.ds(0, count), pl.ds(0, (n - 1) * pc)]
        wait(sem + 1, got, got)

    def product_start(p, panel_c, panel_r, sem):
        ph, plo = split(panel_c)
        both = jnp.concatenate([ph, plo], axis=1)

        def one(a, carry):
            at = pl.multiple_of(a * NB, NB)
            high = ahi[pl.ds(at, NB), :]
            low = alo[pl.ds(at, NB), :]
            wide = mxu(high, both, NN)
            wpart[p, pl.ds(at, NB), :] = wide[:, :NB] + (wide[:, NB:] + mxu(low, ph, NN))
            return carry

        lax.fori_loop(0, tiles, one, 0)
        over_cols(
            sem,
            lambda j: wpart.at[p, pl.ds(j * ch, ch)],
            lambda j: wrs.at[p, c],
        )
        wrs[p, c] = wpart[p, pl.ds(c * ch, ch), :]
        h_src[p] = dot3(panel_r(), wpart[p], TN)
        over_cols(
            sem + 1,
            lambda j: h_src.at[p, pl.ds(j * pc, pc)],
            lambda j: h_slot.at[p, c],
        )
        h_slot[p, c] = h_src[p, pl.ds(c * pc, pc), :]

    def product_mid(p, sem):
        got = wrs.at[p, pl.ds(0, n - 1)]
        wait(sem, got, got)
        total = wrs[p, 0]
        for j in range(1, n):
            total = total + wrs[p, j]
        wch[p] = total

        @pl.when(r != c)
        def _():
            send(wch.at[p], wc.at[p, c // 2, lax.rem(c, 2)], sem + 2, (c, r))

        @pl.when(r == c)
        def _():
            wc[p, level, parity] = total

        wr[p, pl.ds(c * ch, ch), :] = total
        gather_cols_start(wr.at[p], sem + 3)
        got = h_slot.at[p, pl.ds(0, n - 1)]
        wait(sem + 1, got, got)
        total = h_slot[p, 0]
        for j in range(1, n):
            total = total + h_slot[p, j]
        h_piece[p] = total
        over_rows(sem + 6, lambda j: h_piece.at[p], lambda j: h_ex.at[p, r])
        h_ex[p, r] = total

    def product_late(p, sem):
        @pl.when(r != c)
        def _():
            wait(sem + 2, wch.at[p], wc.at[p, level, parity])

        gather_rows_start(wc.at[p], sem + 4)
        got = h_ex.at[p, pl.ds(0, n - 1)]
        wait(sem + 6, got, got)
        total = h_ex[p, 0]
        for j in range(1, n):
            total = total + h_ex[p, j]
        h_res[p, pl.ds(c * pc, pc), :] = total
        mine = h_res.at[p, pl.ds(c * pc, pc)]
        over_cols(sem + 7, lambda j: mine, lambda j: mine)

    def product_wait(p, sem):
        gather_rows_mid(wc.at[p], sem + 4)
        gather_cols_wait(wr.at[p], sem + 3)
        got = h_res.at[p, pl.ds(0, (n - 1) * pc)]
        wait(sem + 7, got, got)
        gather_rows_wait(wc.at[p], sem + 4)

    def flat(ref):
        return ref[...].reshape(rows, NB)

    def core(r_mat, z, h, k, corner):
        kr = exact(k, r_mat)
        s = h + kr + kr.T + exact(exact(r_mat, corner, TN), r_mat)
        return 0.5 * exact(exact(z, s, TN), z), exact(r_mat, z)

    zero_tile = jnp.zeros((NB, NB), jnp.float32)

    load.wait()
    for t in range(3):

        @pl.when(c == t)
        def _():
            for a in range(tiles):
                stg_r[a * NB : (a + 1) * NB, :] = abuf[pl.ds(a * NB * tiles, NB, stride=tiles), :]

            @pl.when(r == 0)
            def _():
                stg_r[0:NB, :] = zero_tile

        @pl.when(r == t)
        def _():
            for b in range(tiles):
                stg_c[b * NB : (b + 1) * NB, :] = abuf[pl.ds(b, NB, stride=tiles), :].T

            @pl.when(c == 0)
            def _():
                stg_c[0:NB, :] = zero_tile

        scatter(t)
    t_ref[...] = zero_tile
    scatter_wait(0)
    gather_rows_start(xc.at[0], 6)
    gather_cols_start(xr.at[0], 8)

    def to_parts(a, carry):
        for b in range(tiles):
            high, low = split(abuf[pl.ds(a * NB * tiles + b, NB, stride=tiles), :])
            at = pl.multiple_of(a * NB, NB)
            ahi[pl.ds(at, NB), b * NB : (b + 1) * NB] = high
            alo[pl.ds(at, NB), b * NB : (b + 1) * NB] = low
        return carry

    lax.fori_loop(0, tiles, to_parts, 0)
    scatter_wait(1)
    scatter_wait(2)
    gather_rows_mid(xc.at[0], 6)
    gather_rows_wait(xc.at[0], 6)
    x0c = flat(xc.at[0])
    first = jnp.where(c == 1, x0c[0:NB], 0.0)
    second = jnp.where(c == 2, x0c[0:NB], 0.0)
    sum_start(0, [dot3(x0c, x0c, TN), first, second], 9)

    def x0r():
        gather_cols_wait(xr.at[0], 8)
        return xr[0]

    product_start(0, x0c, x0r, 20)
    gather_rows_start(xc.at[1], 11)
    gather_cols_start(xr.at[1], 13)
    sum_mid(0, 3, 9)
    sum_wait(0, 3, 9)
    g_ref[...] = ar_res[0, 0]
    cholesky_blocks(g_ref, r0_ref, 0, NB // 8)
    product_mid(0, 20)
    gather_rows_mid(xc.at[1], 11)
    gather_rows_wait(xc.at[1], 11)
    x1c = flat(xc.at[1])
    first = jnp.where(c == 1, x1c[0:NB], 0.0)
    second = jnp.where(c == 2, x1c[0:NB], 0.0)
    sum_start(1, [dot3(flat(xc.at[0]), x1c, TN), first, second], 14)
    y_ref[...] = ar_res[0, 0] + exact(ar_res[0, 1], r0_ref[...], TN)
    product_late(0, 20)
    inverse_blocks(y_ref, t_ref, 0, NB // 16)
    sum_mid(1, 3, 14)
    inverse_blocks(y_ref, t_ref, NB // 16, NB // 8)
    product_wait(0, 20)
    gather_cols_wait(xr.at[1], 13)
    sum_wait(1, 3, 14)
    gather_rows_start(xc.at[2], 16)
    gather_cols_start(xr.at[2], 18)

    r0 = r0_ref[...]
    z0 = y_ref[...]
    k0 = ar_res[1, 0]
    b0, rz0 = core(r0, z0, h_res[0], k0, ar_res[1, 1])
    f01 = ar_res[0, 1] + r0
    f02 = ar_res[0, 2]
    c01 = exact(k0, z0, TN) + exact(ar_res[1, 1], rz0) - exact(f01, b0)
    coef = jnp.concatenate([z0, rz0, -b0], axis=0)
    back = jnp.concatenate([f01, c01], axis=1)

    def first_panel(f_ref, c_ref, p_ref, x0, x1, w, index):
        f_ref[...] = x0

        @pl.when(index == 1)
        def _():
            f_ref[0:NB, :] = f_ref[0:NB, :] + r0

        c_ref[...] = dot3(jnp.concatenate([w, x1, f_ref[...]], axis=1), coef, NN)

        @pl.when(index == 0)
        def _():
            c_ref[0:NB, :] = zero_tile

        left = jnp.concatenate([c_ref[...], f_ref[...]], axis=1)
        p_ref[...] = x1 - dot3(left, back, NT)

        @pl.when(index <= 1)
        def _():
            p_ref[0:NB, :] = zero_tile

    first_panel(f0c, c0c, f1c, flat(xc.at[0]), flat(xc.at[1]), flat(wc.at[0]), c)
    p1c = f1c[...]
    first = jnp.where(c == 2, p1c[0:NB], 0.0)
    left = jnp.concatenate([p1c, f0c[...], c0c[...]], axis=1)
    inner = dot3(left, p1c, TN)
    sum_start(2, [inner[0:NB], inner[NB : 2 * NB], inner[2 * NB :], first], 30)

    def p1r():
        first_panel(f0r, c0r, f1r, xr[0], xr[1], wr[0], r)
        return f1r[...]

    product_start(1, p1c, p1r, 34)
    sum_mid(2, 4, 30)
    sum_wait(2, 4, 30)
    g_ref[...] = ar_res[2, 0]
    cholesky_blocks(g_ref, r1_ref, 0, NB // 8)
    product_mid(1, 34)
    gather_rows_mid(xc.at[2], 16)
    gather_rows_wait(xc.at[2], 16)
    x2c = flat(xc.at[2])
    first = jnp.where(c == 2, x2c[0:NB], 0.0)
    left = jnp.concatenate([flat(xc.at[0]), f1c[...]], axis=1)
    inner = dot3(left, x2c, TN)
    sum_start(3, [inner[0:NB], inner[NB:], first], 32)
    y_ref[...] = ar_res[2, 0] + exact(ar_res[2, 3], r1_ref[...], TN)
    product_late(1, 34)
    inverse_blocks(y_ref, t_ref, 0, NB // 16)
    sum_mid(3, 3, 32)
    inverse_blocks(y_ref, t_ref, NB // 16, NB // 8)
    product_wait(1, 34)
    gather_cols_wait(xr.at[2], 18)
    sum_wait(3, 3, 32)

    r1 = r1_ref[...]
    z1 = y_ref[...]
    j1 = ar_res[2, 1]
    j2 = ar_res[2, 2]
    c02 = exact(ar_res[3, 0], z0, TN) + exact(ar_res[1, 2], rz0) - exact(f02, b0)
    cross = exact(j2, j1, TN)
    cf = exact(c02, f02, NT)
    k1 = ar_res[3, 1] - exact(j2, f02, (((0,), (1,)), ((), ()))) - exact(j1, c02, (((0,), (1,)), ((), ())))
    b1, rz1 = core(r1, z1, h_res[1] - cross - cross.T, k1, ar_res[3, 2] - cf - cf.T)
    coef = jnp.concatenate(
        [
            z1,
            rz1,
            -exact(j1, z1) - exact(f02, rz1, TN),
            -exact(j2, z1) - exact(c02, rz1, TN),
            -b1,
        ],
        axis=0,
    )

    def second_panel(f_ref, c_ref, c0, f0, x2, w, index):
        @pl.when(index == 2)
        def _():
            f_ref[0:NB, :] = f_ref[0:NB, :] + r1

        c_ref[...] = dot3(jnp.concatenate([w, x2, c0, f0, f_ref[...]], axis=1), coef, NN)

        @pl.when(index <= 1)
        def _():
            c_ref[0:NB, :] = zero_tile

    second_panel(f1c, c1c, c0c[...], f0c[...], flat(xc.at[2]), flat(wc.at[1]), c)
    second_panel(f1r, c1r, c0r[...], f0r[...], xr[2], wr[1], r)


def update_kernel(n, tiles, where_ref, a_ref, l0, l1, l2, l3, q0, q1, q2, q3, r0_ref, r1_ref, o_ref, hi, lo):
    a = pl.program_id(0)
    r = where_ref[0]
    c = where_ref[1]

    @pl.when(a == 0)
    def _():
        for i, q in enumerate((q0, q1, q2, q3)):
            high, low = split(q[...])
            hi[:, i * NB : (i + 1) * NB] = high
            lo[:, i * NB : (i + 1) * NB] = low

    lh, ll = split(jnp.concatenate([l0[...], l1[...], l2[...], l3[...]], axis=1))
    change = mxu(lh, hi[...], NT) + (mxu(lh, lo[...], NT) + mxu(ll, hi[...], NT))
    for b in range(tiles):
        at = pl.ds(b, NB, stride=tiles)
        o_ref[at, :] = a_ref[at, :] - change[:, b * NB : (b + 1) * NB]
    row_tile = a * n + r
    zero = jnp.zeros((NB, NB), jnp.float32)
    for p, r_ref in enumerate((r0_ref, r1_ref)):

        @pl.when((c == p) & (row_tile == p + 1))
        def _():
            o_ref[pl.ds(0, NB, stride=tiles), :] = -r_ref[...]

        @pl.when((c == p) & (row_tile > p + 1))
        def _():
            o_ref[pl.ds(0, NB, stride=tiles), :] = zero

        @pl.when(row_tile == p)
        def _():
            for b in range(tiles):
                at = pl.ds(b, NB, stride=tiles)

                @pl.when(b * n + c == p + 1)
                def _():
                    o_ref[at, :] = -r_ref[...].T

                @pl.when(b * n + c > p + 1)
                def _():
                    o_ref[at, :] = zero


def local(hamiltonian):
    tiles = hamiltonian.shape[0]
    n = lax.axis_size("row")
    rows = tiles * NB
    ch = rows // n
    pc = NB // n
    half = n // 2
    f32 = jnp.float32
    block = hamiltonian.reshape(rows * tiles, NB)
    side = jax.ShapeDtypeStruct((rows, NB), f32)
    square = jax.ShapeDtypeStruct((NB, NB), f32)
    vmem = pl.BlockSpec(memory_space=pltpu.VMEM)
    outs = pl.pallas_call(
        functools.partial(reduce_kernel, n, tiles),
        out_shape=[side] * 8 + [square] * 2,
        in_specs=[pl.BlockSpec(memory_space=pl.ANY)],
        out_specs=[vmem] * 10,
        scratch_shapes=[
            pltpu.VMEM((rows * tiles, NB), f32),
            pltpu.VMEM((rows, rows), jnp.bfloat16),
            pltpu.VMEM((rows, rows), jnp.bfloat16),
            pltpu.VMEM((rows, NB), f32),
            pltpu.VMEM((rows, NB), f32),
            pltpu.VMEM((3, rows, NB), f32),
            pltpu.VMEM((3, half, 2, ch, NB), f32),
            pltpu.VMEM((2, rows, NB), f32),
            pltpu.VMEM((2, n, ch, NB), f32),
            pltpu.VMEM((2, ch, NB), f32),
            pltpu.VMEM((2, rows, NB), f32),
            pltpu.VMEM((2, half, 2, ch, NB), f32),
            pltpu.VMEM((4, 4, NB, NB), f32),
            pltpu.VMEM((4, n, 4, pc, NB), f32),
            pltpu.VMEM((4, 4, NB, NB), f32),
            pltpu.VMEM((2, NB, NB), f32),
            pltpu.VMEM((2, n, pc, NB), f32),
            pltpu.VMEM((2, pc, NB), f32),
            pltpu.VMEM((2, n, pc, NB), f32),
            pltpu.VMEM((2, NB, NB), f32),
            pltpu.VMEM((NB, NB), f32),
            pltpu.VMEM((NB, NB), f32),
            pltpu.VMEM((NB, NB), f32),
            pltpu.SemaphoreType.DMA,
            pltpu.SemaphoreType.DMA((42,)),
            pltpu.SemaphoreType.DMA((42,)),
        ],
        compiler_params=pltpu.CompilerParams(
            collective_id=0, has_side_effects=True, vmem_limit_bytes=VMEM_LIMIT
        ),
        name="reduce_panels",
    )(block)
    c0r, f0r, c1r, f1r, c0c, f0c, c1c, f1c, r0, r1 = outs
    where = jnp.stack([lax.axis_index("row"), lax.axis_index("col")]).astype(jnp.int32)
    tile_spec = pl.BlockSpec((NB, NB), lambda a, *_: (a, 0))
    full_spec = pl.BlockSpec((rows, NB), lambda a, *_: (0, 0))
    square_spec = pl.BlockSpec((NB, NB), lambda a, *_: (0, 0))
    block_spec = pl.BlockSpec((NB * tiles, NB), lambda a, *_: (a, 0))
    result = pl.pallas_call(
        functools.partial(update_kernel, n, tiles),
        out_shape=jax.ShapeDtypeStruct((rows * tiles, NB), f32),
        grid_spec=pltpu.PrefetchScalarGridSpec(
            num_scalar_prefetch=1,
            grid=(tiles,),
            in_specs=[block_spec] + [tile_spec] * 4 + [full_spec] * 4 + [square_spec] * 2,
            out_specs=block_spec,
            scratch_shapes=[
                pltpu.VMEM((rows, 4 * NB), jnp.bfloat16),
                pltpu.VMEM((rows, 4 * NB), jnp.bfloat16),
            ],
        ),
        compiler_params=pltpu.CompilerParams(vmem_limit_bytes=VMEM_LIMIT),
        name="update_matrix",
    )(where, block, c0r, f0r, c1r, f1r, f0c, c0c, f1c, c1c, r0, r1)
    return result.reshape(hamiltonian.shape)


def solution(mesh):
    spec = P(None, "row", None, None, "col", None)
    return jax.shard_map(local, mesh=mesh, in_specs=(spec,), out_specs=spec, check_vma=False)
```

time: 2350 us -> 147 us (0.06); the launches traced: 2320 us -> 146 us
  waiting for transfers between devices: 1210 us -> 0 us
  other arithmetic: 820 us -> 0.59 us
  local copies, waits for them, and re-layouts: 209 us -> 0 us
  Pallas kernels: 0 us -> 146 us
  matrix products: 46.7 us -> 0 us
    psum x12 -> x0, waiting for transfers between devices: 1210 us -> none  [the longest x4 434 us: to_columns(): gathered = lax.psum(placed, 'row')]
    another operation x529 -> x1, other arithmetic: 610 us -> 0.59 us  [local(): jnp.stack([lax.axis_index('row'), lax.axis_index('col')]).astype(jnp.int32)]
    mul x512 -> x0, other arithmetic: 164 us -> none  [sweep(): work = work - below[:, None] * after[None, :]]
    dynamic_slice x256 -> x0, local copies, waits for them, and re-layouts: 159 us -> none  [sweep(): column = work[:, column_index] / pivot_row[column_index]]
    pallas_call x0 -> x2, Pallas kernels: none -> 146 us  [the longest x1 132 us: local(): pl.pallas_call(functools.partial(reduce_kernel, n, tiles), out_shape=[sid...]
    dot_general x14 -> x0, matrix products: 40.3 us -> none  [product(): return jnp.dot(first, second, precision=lax.Precision.HIGHEST)]
    while x514 -> x0, local copies, waits for them, and re-layouts: 24.6 us -> none
  transfers between devices with their start and end apart: 12 -> 0, of which waited for: 12 -> 0; matrix products, arithmetic and copies ran while one was open for 1% -> 0% of each run, Pallas kernels for 0% -> 0%
where the time goes in v1:
time: 147 us; the launch traced here: 146 us
  Pallas kernels  146 us (99%)
    pallas_call x1, Pallas kernels, local(): pl.pallas_call(functools.partial(reduce_kernel, n, tiles), out_shape=[sid...  132 us
    pallas_call x1, Pallas kernels, local(): pl.pallas_call(functools.partial(update_kernel, n, tiles), out_shape=jax....  14.1 us

profile of v1, /device:TPU:1, one launch (start us, length us, event | category | flops | bytes accessed | tf_op | source)
XLA Modules:
  0.0 146.4 jit_solution(6338820286813786557)
XLA Ops:
  0.0 0.6 pad_add_fusion.where_ref
  0.6 131.8 %reduce_panels.1 = (f32[1024,128]{1,0:T(8,128)}, f32[1024,128]{1,0:T(8,128)}, f32[1024,128]{1,0:T(8,128)}, f32[1024,128]{1,0:T(8,128)}, f32[1024,128]{1,0:T(8,12...) custom-call(f32[8192,128]{1,0:T(8,128)} %bitcast.6), custom_call_target="tpu_custom_call" | custom-call | tf_op jit(solution)/shard_map/reduce_panels/pallas_call | solution.py:564
  132.4 14.1 %update_matrix.1 = f32[8192,128]{1,0:T(8,128)} custom-call(s32[2]{0:T(128)} %pad_add_fusion.where_ref, f32[8192,128]{1,0:T(8,128)} %bitcast.7, f32[1024,128]{1,0:T(8,128)} %get-tuple-element.15.l0, f32[1024,128]{1,0:T(8,128)} %get-tuple-element.16.l1, f32[1024,128]{1,0:T(8,128)} %get-tuple-element.17.l2, f32[1024,128]{1,0:T(8,128)} %get-tuple-element.18.l3, ...), custom_call_target="tpu_custom_call" | custom-call | tf_op jit(solution)/shard_map/update_matrix/pallas_call | solution.py:608

commit v2 on v1

v2 whole, which is shorter than its diff:
```python
import functools

import jax
import jax.numpy as jnp
from jax import lax
from jax.experimental import pallas as pl
from jax.experimental.pallas import tpu as pltpu
from jax.sharding import PartitionSpec as P

MESH = pl.DeviceIdType.MESH
NB = 128
NN = (((1,), (0,)), ((), ()))
NT = (((1,), (1,)), ((), ()))
TN = (((0,), (0,)), ((), ()))
TT = (((0,), (1,)), ((), ()))
VMEM_LIMIT = 56 << 20


def split(value):
    high = value.astype(jnp.bfloat16)
    low = (value - high.astype(jnp.float32)).astype(jnp.bfloat16)
    return high, low


def mxu(first, second, dims):
    return lax.dot_general(first, second, dims, preferred_element_type=jnp.float32)


def dot3(first, second, dims):
    fh, fl = split(first)
    sh, sl = split(second)
    return mxu(fh, sh, dims) + (mxu(fh, sl, dims) + mxu(fl, sh, dims))


def exact(first, second, dims=NN):
    return lax.dot_general(
        first, second, dims, precision=lax.Precision.HIGHEST, preferred_element_type=jnp.float32
    )


def iota(axis, shape):
    return lax.broadcasted_iota(jnp.int32, shape, axis)


def cholesky_blocks(g_ref, r_ref, first, last):
    sub = iota(0, (8, NB))
    lane = iota(1, (8, NB))

    def block(k, carry):
        base = pl.multiple_of(k * 8, 8)
        x = g_ref[pl.ds(base, 8), :]
        rolled = pltpu.roll(x, lax.rem(NB - base, NB), 1)
        cols = [jnp.broadcast_to(rolled[:, i : i + 1], (8, NB)) for i in range(8)]
        for i in range(8):
            scale = lax.rsqrt(cols[i][i : i + 1, :])
            column = cols[i] * scale
            below = jnp.where(sub > i, column, 0.0)
            row = x[i : i + 1, :] * scale
            x = jnp.where(sub == i, row, x - below * row)
            for m in range(i + 1, 8):
                cols[m] = cols[m] - below * column[m : m + 1, :]
        x = jnp.where(lane >= base + sub, x, 0.0)
        r_ref[pl.ds(base, 8), :] = x
        g_ref[...] -= exact(x, x, TN)
        return carry

    lax.fori_loop(first, last, block, 0)


def inverse_blocks(y_ref, t_ref, first, last):
    sub = iota(0, (8, NB))
    lane = iota(1, (8, NB))
    wide = iota(1, (NB, NB))

    def block(k, carry):
        base = pl.multiple_of(k * 8, 8)
        x = y_ref[pl.ds(base, 8), :]
        rolled = pltpu.roll(x, lax.rem(NB - base, NB), 1)
        cols = [jnp.broadcast_to(rolled[:, i : i + 1], (8, NB)) for i in range(8)]
        inside = (lane >= base) & (lane < base + 8)
        x = jnp.where(inside, jnp.where(lane - base == sub, 1.0, 0.0), x)
        for i in range(8):
            scale = 1.0 / cols[i][i : i + 1, :]
            factor = jnp.where(sub == i, 0.0, cols[i])
            row = x[i : i + 1, :] * scale
            x = jnp.where(sub == i, row, x - factor * row)
            for m in range(i + 1, 8):
                entry = cols[m][i : i + 1, :] * scale
                cols[m] = jnp.where(sub == i, entry, cols[m] - factor * entry)
        t_ref[pl.ds(base, 8), :] = x
        y = y_ref[...]
        chosen = (wide >= base) & (wide < base + 8)
        y_ref[...] = jnp.where(chosen, 0.0, y) - exact(jnp.where(chosen, y, 0.0), t_ref[...])
        y_ref[pl.ds(base, 8), :] = x
        t_ref[pl.ds(base, 8), :] = jnp.zeros((8, NB), jnp.float32)
        return carry

    lax.fori_loop(first, last, block, 0)


def reduce_kernel(n, tiles, *refs):
    rows = tiles * NB
    ch = rows // n
    pc = NB // n
    half = n // 2
    per_tile = NB // ch
    (
        a_hbm, out_hbm,
        abuf, ahi, alo, thi, tlo, stg_r, stg_c, xr, xc,
        wpart_r, wslot_r, wpart_c, wsib, wsum, wslot_c, wch, wr, wc,
        panel_r, panel_c, cor_r, cor_c, lh, ll, qh, ql,
        ar_src, ar_slot, ar_res, h_src, h_slot, h_piece, h_ex, h_res,
        g_ref, y_ref, t_ref, r0_ref, r1_ref, asem, osem, ss, rs,
    ) = refs
    r = lax.axis_index("row")
    c = lax.axis_index("col")
    parity = lax.rem(r, 2)
    level = r // 2
    sibling = (r + 1 - 2 * parity, c)

    load = pltpu.make_async_copy(a_hbm, abuf, asem)
    load.start()
    barrier = pltpu.get_barrier_semaphore()

    def greet(k, carry):
        pl.semaphore_signal(barrier, inc=1, device_id=(lax.rem(r + k, n), c), device_id_type=MESH)
        pl.semaphore_signal(barrier, inc=1, device_id=(r, lax.rem(c + k, n)), device_id_type=MESH)
        return carry

    lax.fori_loop(1, n, greet, 0)

    @pl.when(r != c)
    def _():
        pl.semaphore_signal(barrier, inc=1, device_id=(c, r), device_id_type=MESH)

    def send(src, dst, sem, device):
        pltpu.make_async_remote_copy(
            src, dst, ss.at[sem], rs.at[sem], device_id=device, device_id_type=MESH
        ).start()

    def over_cols(sem, src_of, dst_of):
        def one(k, carry):
            j = lax.rem(c + k, n)
            send(src_of(j), dst_of(j), sem, (r, j))
            return carry

        lax.fori_loop(1, n, one, 0)

    def over_rows(sem, src_of, dst_of):
        def one(k, carry):
            j = lax.rem(r + k, n)
            send(src_of(j), dst_of(j), sem, (j, c))
            return carry

        lax.fori_loop(1, n, one, 0)

    def wait_sent(sem, sent):
        pltpu.make_async_copy(sent, sent, ss.at[sem]).wait()

    def wait_received(sem, received):
        pltpu.make_async_copy(received, received, rs.at[sem]).wait()

    def wait(sem, part):
        wait_received(sem, part)
        wait_sent(sem, part)

    def scatter(t):
        @pl.when(c == t)
        def _():
            over_cols(
                t,
                lambda j: stg_r.at[pl.ds(j * ch, ch)],
                lambda j: xr.at[t, pl.ds(j * ch, ch)],
            )
            xr[t, pl.ds(t * ch, ch), :] = stg_r[pl.ds(t * ch, ch), :]

        @pl.when(r == t)
        def _():
            over_rows(
                3 + t,
                lambda j: stg_c.at[pl.ds(j * ch, ch)],
                lambda j: xc.at[t, j // 2, lax.rem(j, 2)],
            )
            xc[t, t // 2, t % 2] = stg_c[pl.ds(t * ch, ch), :]

    def scatter_wait(t):
        @pl.when(c == t)
        def _():
            wait_sent(t, stg_r.at[pl.ds(0, (n - 1) * ch)])

        @pl.when(c != t)
        def _():
            wait_received(t, xr.at[t, pl.ds(c * ch, ch)])

        @pl.when(r == t)
        def _():
            wait_sent(3 + t, stg_c.at[pl.ds(0, (n - 1) * ch)])

        @pl.when(r != t)
        def _():
            wait_received(3 + t, xc.at[t, level, parity])

    def gather_cols_start(buf, sem):
        mine = buf.at[pl.ds(c * ch, ch)]
        over_cols(sem, lambda j: mine, lambda j: mine)

    def gather_cols_wait(buf, sem):
        wait(sem, buf.at[pl.ds(0, (n - 1) * ch)])

    def gather_rows_start(buf, sem):
        mine = buf.at[level, parity]

        def one(k, carry):
            send(mine, mine, sem, (lax.rem(level + k, half) * 2 + parity, c))
            return carry

        lax.fori_loop(1, half, one, 0)

    def gather_rows_mid(buf, sem):
        wait(sem, buf.at[pl.ds(0, half - 1), 0])
        mine = buf.at[:, parity]
        send(mine, mine, sem + 1, sibling)

    def gather_rows_wait(buf, sem):
        wait(sem + 1, buf.at[:, 0])

    def sum_start(q, parts, sem, over, me):
        count = len(parts)
        for i, part in enumerate(parts):
            ar_src[q, i] = part
        over(
            sem,
            lambda j: ar_src.at[q, pl.ds(0, count), pl.ds(j * pc, pc)],
            lambda j: ar_slot.at[q, me, pl.ds(0, count)],
        )
        ar_slot[q, me, 0:count] = ar_src[q, 0:count, pl.ds(me * pc, pc), :]

    def sum_slots(q, count, sem):
        wait(sem, ar_slot.at[q, pl.ds(0, n - 1), pl.ds(0, count)])
        total = ar_slot[q, 0, 0:count]
        for j in range(1, n):
            total = total + ar_slot[q, j, 0:count]
        return total

    def sum_spread(q, count, sem, over, me):
        mine = (q, pl.ds(0, count), pl.ds(me * pc, pc))
        over(sem + 1, lambda j: ar_res.at[mine], lambda j: ar_res.at[mine])

    def sum_mid(q, count, sem, over, me):
        ar_res[q, 0:count, pl.ds(me * pc, pc), :] = sum_slots(q, count, sem)
        sum_spread(q, count, sem, over, me)

    def sum_wait(q, count, sem):
        wait(sem + 1, ar_res.at[q, pl.ds(0, count), pl.ds(0, (n - 1) * pc)])

    def all_start(p, part, sem, over, me):
        h_src[p] = part
        over(sem, lambda j: h_src.at[p, pl.ds(j * pc, pc)], lambda j: h_slot.at[p, me])
        h_slot[p, me] = h_src[p, pl.ds(me * pc, pc), :]

    def all_mid(p, sem, over, me):
        wait(sem, h_slot.at[p, pl.ds(0, n - 1)])
        total = h_slot[p, 0]
        for j in range(1, n):
            total = total + h_slot[p, j]
        h_piece[p] = total
        over(sem + 1, lambda j: h_piece.at[p], lambda j: h_ex.at[p, me])
        h_ex[p, me] = total

    def all_late(p, sem, over, me):
        wait(sem + 1, h_ex.at[p, pl.ds(0, n - 1)])
        total = h_ex[p, 0]
        for j in range(1, n):
            total = total + h_ex[p, j]
        h_res[p, pl.ds(me * pc, pc), :] = total
        mine = h_res.at[p, pl.ds(me * pc, pc)]
        over(sem + 2, lambda j: mine, lambda j: mine)

    def all_wait(p, sem):
        wait(sem + 2, h_res.at[p, pl.ds(0, (n - 1) * pc)])

    def tile_product(high_ref, low_ref, at, both):
        wide = mxu(high_ref[pl.ds(at, NB), :], both, NN)
        return wide[:, :NB] + (wide[:, NB:] + mxu(low_ref[pl.ds(at, NB), :], both[:, :NB], NN))

    def halves(panel):
        return jnp.concatenate(split(panel), axis=1)

    def flat(ref):
        return ref[...].reshape(rows, NB)

    def flip(value):
        return jnp.concatenate(
            [value[i * NB : (i + 1) * NB].T for i in range(tiles)], axis=1
        )

    def core(r_mat, z, h, k, corner):
        kr = exact(k, r_mat)
        s = h + kr + kr.T + exact(exact(r_mat, corner, TN), r_mat)
        return 0.5 * exact(exact(z, s, TN), z)

    zero_tile = jnp.zeros((NB, NB), jnp.float32)
    block_rows = min(rows, 2 * NB)

    def keep_left(i, value):
        lh[:, i * NB : (i + 1) * NB], ll[:, i * NB : (i + 1) * NB] = split(value)

    def keep_right(i, value):
        qh[i * NB : (i + 1) * NB, :], ql[i * NB : (i + 1) * NB, :] = split(flip(value))

    def apply(p, finish):
        depth = slice(2 * p * NB, 2 * (p + 1) * NB)

        def one(i, carry):
            at = pl.multiple_of(i * block_rows, block_rows)
            high = lh[pl.ds(at, block_rows), depth]
            low = ll[pl.ds(at, block_rows), depth]
            for b in range(0, tiles, 2):
                cols = slice(b * NB, (b + 2) * NB)
                change = mxu(high, qh[depth, cols], NN) + (
                    mxu(high, ql[depth, cols], NN) + mxu(low, qh[depth, cols], NN)
                )
                for k in range(block_rows // NB):
                    for j in range(2):
                        spot = pl.ds((at + k * NB) * tiles + b + j, NB, stride=tiles)
                        part = change[k * NB : (k + 1) * NB, j * NB : (j + 1) * NB]
                        abuf[spot, :] = abuf[spot, :] - part
            if finish:
                area = pl.ds(pl.multiple_of(at * tiles, block_rows), block_rows * tiles)
                pltpu.make_async_copy(abuf.at[area], out_hbm.at[area], osem).start()
            return carry

        lax.fori_loop(0, rows // block_rows, one, 0)

    def write_band(p, r_ref):
        @pl.when(c == p)
        def _():
            for a in range(tiles):
                spot = pl.ds(a * NB * tiles, NB, stride=tiles)

                @pl.when(a * n + r == p + 1)
                def _():
                    abuf[spot, :] = -r_ref[...]

                @pl.when(a * n + r > p + 1)
                def _():
                    abuf[spot, :] = zero_tile

        @pl.when(r == p)
        def _():
            for b in range(tiles):
                spot = pl.ds(b, NB, stride=tiles)

                @pl.when(b * n + c == p + 1)
                def _():
                    abuf[spot, :] = -r_ref[...].T

                @pl.when(b * n + c > p + 1)
                def _():
                    abuf[spot, :] = zero_tile

    load.wait()
    for t in range(3):

        @pl.when(c == t)
        def _():
            for a in range(tiles):
                stg_r[a * NB : (a + 1) * NB, :] = abuf[pl.ds(a * NB * tiles, NB, stride=tiles), :]

            @pl.when(r == 0)
            def _():
                stg_r[0:NB, :] = zero_tile

        @pl.when(r == t)
        def _():
            for b in range(tiles):
                stg_c[b * NB : (b + 1) * NB, :] = abuf[pl.ds(b, NB, stride=tiles), :].T

            @pl.when(c == 0)
            def _():
                stg_c[0:NB, :] = zero_tile

    pl.semaphore_wait(barrier, 2 * (n - 1) + jnp.where(r != c, 1, 0))
    for t in range(3):
        scatter(t)

    @pl.when(r == 0)
    def _():
        mine = stg_c[...]
        first = jnp.where(c == 1, mine[0:NB], 0.0)
        second = jnp.where(c == 2, mine[0:NB], 0.0)
        sum_start(0, [dot3(mine, mine, TN), first, second], 9, over_cols, c)

    t_ref[...] = zero_tile
    scatter_wait(0)
    gather_rows_start(xc.at[0], 6)

    g_mine = (0, pl.ds(0, 3), pl.ds(c * pc, pc))

    @pl.when(r == 0)
    def _():
        ar_res[0, 0:3, pl.ds(c * pc, pc), :] = sum_slots(0, 3, 9)
        over_rows(19, lambda j: ar_res.at[g_mine], lambda j: ar_res.at[g_mine])

    gather_cols_start(xr.at[0], 8)

    def to_parts(a, carry):
        at = pl.multiple_of(a * NB, NB)
        for b in range(tiles):
            high, low = split(abuf[pl.ds(a * NB * tiles + b, NB, stride=tiles), :])
            ahi[pl.ds(at, NB), b * NB : (b + 1) * NB] = high
            alo[pl.ds(at, NB), b * NB : (b + 1) * NB] = low
        return carry

    lax.fori_loop(0, tiles, to_parts, 0)

    @pl.when(r == 0)
    def _():
        wait_sent(19, ar_res.at[0, pl.ds(0, 3), pl.ds(0, (n - 1) * pc)])

    @pl.when(r != 0)
    def _():
        wait_received(19, ar_res.at[g_mine])

    sum_spread(0, 3, 9, over_cols, c)
    scatter_wait(1)
    gather_cols_start(xr.at[1], 13)
    scatter_wait(2)

    def to_flipped(b, carry):
        at = pl.multiple_of(b * NB, NB)
        for a in range(tiles):
            high, low = split(abuf[pl.ds(a * NB * tiles + b, NB, stride=tiles), :].T)
            thi[pl.ds(at, NB), a * NB : (a + 1) * NB] = high
            tlo[pl.ds(at, NB), a * NB : (a + 1) * NB] = low
        return carry

    lax.fori_loop(0, tiles, to_flipped, 0)
    gather_rows_mid(xc.at[0], 6)
    gather_rows_wait(xc.at[0], 6)

    both = halves(flat(xc.at[0]))

    def first_product(a, carry):
        at = pl.multiple_of(a * NB, NB)
        wpart_r[pl.ds(at, NB), :] = tile_product(ahi, alo, at, both)
        for i in range(per_tile):
            j = a * per_tile + i
            mine = wpart_r.at[pl.ds(j * ch, ch)]

            @pl.when(j != c)
            def _():
                send(mine, wslot_r.at[c], 20, (r, j))

        return carry

    lax.fori_loop(0, tiles, first_product, 0)
    wslot_r[c] = wpart_r[pl.ds(c * ch, ch), :]
    gather_rows_start(xc.at[1], 11)
    gather_cols_wait(xr.at[0], 8)
    all_start(0, dot3(xr[0], wpart_r[...], TN), 26, over_rows, r)
    gather_cols_wait(xr.at[1], 13)
    first = jnp.where(r == 1, xr[1, 0:NB], 0.0)
    second = jnp.where(r == 2, xr[1, 0:NB], 0.0)
    sum_start(1, [dot3(xr[0], xr[1], TN), first, second], 14, over_rows, r)
    sum_wait(0, 3, 9)
    g_ref[...] = ar_res[0, 0]
    cholesky_blocks(g_ref, r0_ref, 0, NB // 16)
    all_mid(0, 26, over_cols, c)
    sum_mid(1, 3, 14, over_rows, r)
    gather_rows_mid(xc.at[1], 11)
    gather_rows_start(xc.at[2], 16)
    cholesky_blocks(g_ref, r0_ref, NB // 16, NB // 8)

    wait(20, wslot_r.at[pl.ds(0, n - 1)])
    total = wslot_r[0]
    for j in range(1, n):
        total = total + wslot_r[j]
    wr[0, pl.ds(c * ch, ch), :] = total
    gather_cols_start(wr.at[0], 23)
    wch[0] = total

    @pl.when(r != c)
    def _():
        send(wch.at[0], wc.at[0, c // 2, lax.rem(c, 2)], 22, (c, r))

    @pl.when(r == c)
    def _():
        wc[0, level, parity] = total

    all_late(0, 26, over_rows, r)
    y_ref[...] = ar_res[0, 0] + exact(ar_res[0, 1], r0_ref[...], TN)
    inverse_blocks(y_ref, t_ref, 0, 3 * NB // 32)
    sum_wait(1, 3, 14)
    gather_rows_mid(xc.at[2], 16)

    @pl.when(r != c)
    def _():
        wait_received(22, wc.at[0, level, parity])
        wait_sent(22, wch.at[0])

    gather_rows_start(wc.at[0], 24)
    inverse_blocks(y_ref, t_ref, 3 * NB // 32, NB // 8)
    r0 = r0_ref[...]
    z0 = y_ref[...]
    k0 = ar_res[1, 0]
    rz0 = exact(r0, z0)
    f01 = ar_res[0, 1] + r0
    f02 = ar_res[0, 2]
    all_wait(0, 26)
    b0 = core(r0, z0, h_res[0], k0, ar_res[1, 1])
    c01 = exact(k0, z0, TN) + exact(ar_res[1, 1], rz0) - exact(f01, b0)
    coef = jnp.concatenate([z0, rz0, -b0], axis=0)
    back = jnp.concatenate([f01, c01], axis=1)

    def first_panel(f_ref, c_ref, x0, x1, w, index):
        f_ref[0] = x0

        @pl.when(index == 1)
        def _():
            f_ref[0, 0:NB, :] = f_ref[0, 0:NB, :] + r0

        c_ref[0] = dot3(jnp.concatenate([w, x1, f_ref[0]], axis=1), coef, NN)

        @pl.when(index == 0)
        def _():
            c_ref[0, 0:NB, :] = zero_tile

        left = jnp.concatenate([c_ref[0], f_ref[0]], axis=1)
        f_ref[1] = x1 - dot3(left, back, NT)

        @pl.when(index <= 1)
        def _():
            f_ref[1, 0:NB, :] = zero_tile

    gather_cols_wait(wr.at[0], 23)
    gather_cols_start(xr.at[2], 18)
    first_panel(panel_r, cor_r, xr[0], xr[1], wr[0], r)

    p1r = panel_r[1]
    first = jnp.where(r == 2, p1r[0:NB], 0.0)
    inner = dot3(jnp.concatenate([p1r, panel_r[0], cor_r[0]], axis=1), p1r, TN)
    sum_start(2, [inner[0:NB], inner[NB : 2 * NB], inner[2 * NB :], first], 30, over_rows, r)
    both = halves(p1r)

    def second_product(b, carry):
        at = pl.multiple_of(b * NB, NB)
        value = tile_product(thi, tlo, at, both).reshape(per_tile, ch, NB)
        for i in range(per_tile):
            j = b * per_tile + i
            wpart_c[j // 2, lax.rem(j, 2)] = value[i]
        return carry

    lax.fori_loop(0, tiles, second_product, 0)
    send(wpart_c.at[:, 1 - parity], wsib, 34, sibling)
    gather_rows_mid(wc.at[0], 24)
    sum_mid(2, 4, 30, over_rows, r)
    wait(34, wsib)
    wsum[...] = wpart_c[:, parity] + wsib[...]

    def spread(k, carry):
        to = lax.rem(level + k, half)
        send(wsum.at[to], wslot_c.at[level], 35, (to * 2 + parity, c))
        return carry

    lax.fori_loop(1, half, spread, 0)
    wslot_c[level] = wsum[level]
    gather_rows_wait(xc.at[1], 11)
    gather_rows_wait(xc.at[2], 16)
    gather_rows_wait(wc.at[0], 24)
    first_panel(panel_c, cor_c, flat(xc.at[0]), flat(xc.at[1]), flat(wc.at[0]), c)
    p1c = panel_c[1]
    all_start(1, dot3(p1c, flat(wpart_c), TN), 36, over_cols, c)
    x2c = flat(xc.at[2])
    first = jnp.where(c == 2, x2c[0:NB], 0.0)
    inner = dot3(jnp.concatenate([flat(xc.at[0]), p1c], axis=1), x2c, TN)
    sum_start(3, [inner[0:NB], inner[NB:], first], 32, over_cols, c)
    keep_left(0, cor_r[0])
    keep_left(1, panel_r[0])
    keep_right(0, panel_c[0])
    keep_right(1, cor_c[0])
    sum_wait(2, 4, 30)
    g_ref[...] = ar_res[2, 0]
    cholesky_blocks(g_ref, r1_ref, 0, NB // 16)

    wait(35, wslot_c.at[pl.ds(0, half - 1)])
    total = wslot_c[0]
    for j in range(1, half):
        total = total + wslot_c[j]
    wc[1, level, parity] = total
    gather_rows_start(wc.at[1], 39)
    wch[1] = total

    @pl.when(r != c)
    def _():
        send(wch.at[1], wr.at[1, pl.ds(r * ch, ch)], 41, (c, r))

    @pl.when(r == c)
    def _():
        wr[1, pl.ds(c * ch, ch), :] = total

    all_mid(1, 36, over_rows, r)
    sum_mid(3, 3, 32, over_cols, c)
    cholesky_blocks(g_ref, r1_ref, NB // 16, NB // 8)
    all_late(1, 36, over_cols, c)
    y_ref[...] = ar_res[2, 0] + exact(ar_res[2, 3], r1_ref[...], TN)

    @pl.when(r != c)
    def _():
        wait_received(41, wr.at[1, pl.ds(c * ch, ch)])
        wait_sent(41, wch.at[1])

    gather_cols_start(wr.at[1], 42)
    inverse_blocks(y_ref, t_ref, 0, NB // 16)
    gather_rows_mid(wc.at[1], 39)
    inverse_blocks(y_ref, t_ref, NB // 16, NB // 8)
    apply(0, False)
    write_band(0, r0_ref)
    write_band(1, r1_ref)
    r1 = r1_ref[...]
    z1 = y_ref[...]
    j1 = ar_res[2, 1]
    j2 = ar_res[2, 2]
    rz1 = exact(r1, z1)
    sum_wait(3, 3, 32)
    c02 = exact(ar_res[3, 0], z0, TN) + exact(ar_res[1, 2], rz0) - exact(f02, b0)
    cross = exact(j2, j1, TN)
    cf = exact(c02, f02, NT)
    k1 = ar_res[3, 1] - exact(j2, f02, TT) - exact(j1, c02, TT)
    fold1 = -exact(j1, z1) - exact(f02, rz1, TN)
    fold2 = -exact(j2, z1) - exact(c02, rz1, TN)
    all_wait(1, 36)
    b1 = core(r1, z1, h_res[1] - cross - cross.T, k1, ar_res[3, 2] - cf - cf.T)
    coef = jnp.concatenate([z1, rz1, fold1, fold2, -b1], axis=0)

    def second_panel(f_ref, c_ref, x2, w, index):
        @pl.when(index == 2)
        def _():
            f_ref[1, 0:NB, :] = f_ref[1, 0:NB, :] + r1

        c_ref[1] = dot3(jnp.concatenate([w, x2, c_ref[0], f_ref[0], f_ref[1]], axis=1), coef, NN)

        @pl.when(index <= 1)
        def _():
            c_ref[1, 0:NB, :] = zero_tile

    gather_rows_wait(wc.at[1], 39)
    second_panel(panel_c, cor_c, flat(xc.at[2]), flat(wc.at[1]), c)
    keep_right(2, panel_c[1])
    keep_right(3, cor_c[1])
    gather_cols_wait(xr.at[2], 18)
    gather_cols_wait(wr.at[1], 42)
    second_panel(panel_r, cor_r, xr[2], wr[1], r)
    keep_left(2, cor_r[1])
    keep_left(3, panel_r[1])
    apply(1, True)
    pltpu.make_async_copy(abuf, out_hbm, osem).wait()


def local(hamiltonian):
    tiles = hamiltonian.shape[0]
    n = lax.axis_size("row")
    rows = tiles * NB
    ch = rows // n
    pc = NB // n
    half = n // 2
    f32 = jnp.float32
    bf16 = jnp.bfloat16
    block = hamiltonian.reshape(rows * tiles, NB)
    shapes = [
        ((rows * tiles, NB), f32),
        ((rows, rows), bf16),
        ((rows, rows), bf16),
        ((rows, rows), bf16),
        ((rows, rows), bf16),
        ((rows, NB), f32),
        ((rows, NB), f32),
        ((3, rows, NB), f32),
        ((3, half, 2, ch, NB), f32),
        ((rows, NB), f32),
        ((n, ch, NB), f32),
        ((half, 2, ch, NB), f32),
        ((half, ch, NB), f32),
        ((half, ch, NB), f32),
        ((half, ch, NB), f32),
        ((2, ch, NB), f32),
        ((2, rows, NB), f32),
        ((2, half, 2, ch, NB), f32),
        ((2, rows, NB), f32),
        ((2, rows, NB), f32),
        ((2, rows, NB), f32),
        ((2, rows, NB), f32),
        ((rows, 4 * NB), bf16),
        ((rows, 4 * NB), bf16),
        ((4 * NB, rows), bf16),
        ((4 * NB, rows), bf16),
        ((4, 4, NB, NB), f32),
        ((4, n, 4, pc, NB), f32),
        ((4, 4, NB, NB), f32),
        ((2, NB, NB), f32),
        ((2, n, pc, NB), f32),
        ((2, pc, NB), f32),
        ((2, n, pc, NB), f32),
        ((2, NB, NB), f32),
    ] + [((NB, NB), f32)] * 5
    result = pl.pallas_call(
        functools.partial(reduce_kernel, n, tiles),
        out_shape=jax.ShapeDtypeStruct((rows * tiles, NB), f32),
        in_specs=[pl.BlockSpec(memory_space=pl.ANY)],
        out_specs=pl.BlockSpec(memory_space=pl.ANY),
        scratch_shapes=[pltpu.VMEM(*shape) for shape in shapes]
        + [
            pltpu.SemaphoreType.DMA,
            pltpu.SemaphoreType.DMA,
            pltpu.SemaphoreType.DMA((43,)),
            pltpu.SemaphoreType.DMA((43,)),
        ],
        compiler_params=pltpu.CompilerParams(
            collective_id=0, has_side_effects=True, vmem_limit_bytes=VMEM_LIMIT
        ),
        name="reduce_panels",
    )(block)
    return result.reshape(hamiltonian.shape)


def solution(mesh):
    spec = P(None, "row", None, None, "col", None)
    return jax.shard_map(local, mesh=mesh, in_specs=(spec,), out_specs=spec, check_vma=False)
```

time: 147 us -> 135 us (0.918)
  Pallas kernels: 146 us -> 128 us
  local copies, waits for them, and re-layouts: 0 us -> 7.08 us
    pallas_call x2 -> x1, Pallas kernels: 146 us -> 128 us  [local(): pl.pallas_call(functools.partial(reduce_kernel, n, tiles), out_shape=jax....]
    unnamed x0 -> x1, local copies, waits for them, and re-layouts: none -> 7.08 us
where the time goes in v2:
time: 135 us
  Pallas kernels  128 us (95%)
  local copies, waits for them, and re-layouts  7.08 us (5%)
    pallas_call x1, Pallas kernels, local(): pl.pallas_call(functools.partial(reduce_kernel, n, tiles), out_shape=jax....  128 us
    unnamed x1, local copies, waits for them, and re-layouts  7.08 us

profile of v2, /device:TPU:1, one launch (start us, length us, event | category | flops | bytes accessed | tf_op | source)
XLA Modules:
  0.0 135.3 jit_solution(4143342229782985467)
XLA Ops:
  0.0 128.2 %reduce_panels.1 = f32[8192,128]{1,0:T(8,128)} custom-call(f32[8192,128]{1,0:T(8,128)} %bitcast.5), custom_call_target="tpu_custom_call" | custom-call | tf_op jit(solution)/shard_map/reduce_panels/pallas_call | solution.py:706
  128.2 7.1 %copy.4 = f32[8,1,128,8,1,128]{5,4,3,2,1,0:T(1,128)} copy(f32[8,1,128,8,1,128]{5,4,3,2,1,0:T(1,128)} %bitcast.4) | data formatting | bytes 8388608

commit v3 on v2

--- a/solution.py
+++ b/solution.py
@@ -14,6 +14,10 @@
 TN = (((0,), (0,)), ((), ()))
 TT = (((0,), (1,)), ((), ()))
 VMEM_LIMIT = 56 << 20
+CHOL_WIDTH = 32
+INV_WIDTH = 16
+CHOL_BLOCKS = NB // CHOL_WIDTH
+INV_BLOCKS = NB // INV_WIDTH
 
 
 def split(value):
@@ -42,25 +46,30 @@
     return lax.broadcasted_iota(jnp.int32, shape, axis)
 
 
+def leading_columns(x, base, width):
+    rolled = pltpu.roll(x, lax.rem(NB - base, NB), 1)
+    return [jnp.broadcast_to(rolled[:, i : i + 1], (width, NB)) for i in range(width)]
+
+
 def cholesky_blocks(g_ref, r_ref, first, last):
-    sub = iota(0, (8, NB))
-    lane = iota(1, (8, NB))
+    width = CHOL_WIDTH
+    sub = iota(0, (width, NB))
+    lane = iota(1, (width, NB))
 
     def block(k, carry):
-        base = pl.multiple_of(k * 8, 8)
-        x = g_ref[pl.ds(base, 8), :]
-        rolled = pltpu.roll(x, lax.rem(NB - base, NB), 1)
-        cols = [jnp.broadcast_to(rolled[:, i : i + 1], (8, NB)) for i in range(8)]
-        for i in range(8):
+        base = pl.multiple_of(k * width, width)
+        x = g_ref[pl.ds(base, width), :]
+        cols = leading_columns(x, base, width)
+        for i in range(width):
             scale = lax.rsqrt(cols[i][i : i + 1, :])
             column = cols[i] * scale
             below = jnp.where(sub > i, column, 0.0)
             row = x[i : i + 1, :] * scale
             x = jnp.where(sub == i, row, x - below * row)
-            for m in range(i + 1, 8):
+            for m in range(i + 1, width):
                 cols[m] = cols[m] - below * column[m : m + 1, :]
         x = jnp.where(lane >= base + sub, x, 0.0)
-        r_ref[pl.ds(base, 8), :] = x
+        r_ref[pl.ds(base, width), :] = x
         g_ref[...] -= exact(x, x, TN)
         return carry
 
@@ -68,31 +77,31 @@
 
 
 def inverse_blocks(y_ref, t_ref, first, last):
-    sub = iota(0, (8, NB))
-    lane = iota(1, (8, NB))
+    width = INV_WIDTH
+    sub = iota(0, (width, NB))
+    lane = iota(1, (width, NB))
     wide = iota(1, (NB, NB))
 
     def block(k, carry):
-        base = pl.multiple_of(k * 8, 8)
-        x = y_ref[pl.ds(base, 8), :]
-        rolled = pltpu.roll(x, lax.rem(NB - base, NB), 1)
-        cols = [jnp.broadcast_to(rolled[:, i : i + 1], (8, NB)) for i in range(8)]
-        inside = (lane >= base) & (lane < base + 8)
+        base = pl.multiple_of(k * width, width)
+        x = y_ref[pl.ds(base, width), :]
+        cols = leading_columns(x, base, width)
+        inside = (lane >= base) & (lane < base + width)
         x = jnp.where(inside, jnp.where(lane - base == sub, 1.0, 0.0), x)
-        for i in range(8):
+        for i in range(width):
             scale = 1.0 / cols[i][i : i + 1, :]
             factor = jnp.where(sub == i, 0.0, cols[i])
             row = x[i : i + 1, :] * scale
             x = jnp.where(sub == i, row, x - factor * row)
-            for m in range(i + 1, 8):
+            for m in range(i + 1, width):
                 entry = cols[m][i : i + 1, :] * scale
                 cols[m] = jnp.where(sub == i, entry, cols[m] - factor * entry)
-        t_ref[pl.ds(base, 8), :] = x
+        t_ref[pl.ds(base, width), :] = x
         y = y_ref[...]
-        chosen = (wide >= base) & (wide < base + 8)
+        chosen = (wide >= base) & (wide < base + width)
         y_ref[...] = jnp.where(chosen, 0.0, y) - exact(jnp.where(chosen, y, 0.0), t_ref[...])
-        y_ref[pl.ds(base, 8), :] = x
-        t_ref[pl.ds(base, 8), :] = jnp.zeros((8, NB), jnp.float32)
+        y_ref[pl.ds(base, width), :] = x
+        t_ref[pl.ds(base, width), :] = jnp.zeros((width, NB), jnp.float32)
         return carry
 
     lax.fori_loop(first, last, block, 0)
@@ -105,12 +114,12 @@
     half = n // 2
     per_tile = NB // ch
     (
-        a_hbm, out_hbm,
+        a_hbm, a_out, lh_out, ll_out, qh_out, ql_out,
         abuf, ahi, alo, thi, tlo, stg_r, stg_c, xr, xc,
         wpart_r, wslot_r, wpart_c, wsib, wsum, wslot_c, wch, wr, wc,
         panel_r, panel_c, cor_r, cor_c, lh, ll, qh, ql,
         ar_src, ar_slot, ar_res, h_src, h_slot, h_piece, h_ex, h_res,
-        g_ref, y_ref, t_ref, r0_ref, r1_ref, asem, osem, ss, rs,
+        g_ref, y_ref, t_ref, r0_ref, r1_ref, asem, osem, osem2, osem3, osem4, ss, rs,
     ) = refs
     r = lax.axis_index("row")
     c = lax.axis_index("col")
@@ -294,40 +303,41 @@
             [value[i * NB : (i + 1) * NB].T for i in range(tiles)], axis=1
         )
 
-    def core(r_mat, z, h, k, corner):
+    def known_part(r_mat, k, corner):
         kr = exact(k, r_mat)
-        s = h + kr + kr.T + exact(exact(r_mat, corner, TN), r_mat)
-        return 0.5 * exact(exact(z, s, TN), z)
+        return kr + kr.T + exact(exact(r_mat, corner, TN), r_mat)
+
+    def core(z, inner_sum):
+        return 0.5 * exact(exact(z, inner_sum, TN), z)
 
     zero_tile = jnp.zeros((NB, NB), jnp.float32)
     block_rows = min(rows, 2 * NB)
 
-    def keep_left(i, value):
-        lh[:, i * NB : (i + 1) * NB], ll[:, i * NB : (i + 1) * NB] = split(value)
-
-    def keep_right(i, value):
-        qh[i * NB : (i + 1) * NB, :], ql[i * NB : (i + 1) * NB, :] = split(flip(value))
-
-    def apply(p, finish):
-        depth = slice(2 * p * NB, 2 * (p + 1) * NB)
-
+    def keep_left(p, first, second):
+        for i, value in enumerate((first, second)):
+            spot = slice(i * NB, (i + 1) * NB)
+            lh[p, :, spot], ll[p, :, spot] = split(value)
+
+    def keep_right(p, first, second):
+        for i, value in enumerate((first, second)):
+            spot = slice(i * NB, (i + 1) * NB)
+            qh[p, spot, :], ql[p, spot, :] = split(flip(value))
+
+    def apply_first():
         def one(i, carry):
             at = pl.multiple_of(i * block_rows, block_rows)
-            high = lh[pl.ds(at, block_rows), depth]
-            low = ll[pl.ds(at, block_rows), depth]
+            high = lh[0, pl.ds(at, block_rows)]
+            low = ll[0, pl.ds(at, block_rows)]
             for b in range(0, tiles, 2):
                 cols = slice(b * NB, (b + 2) * NB)
-                change = mxu(high, qh[depth, cols], NN) + (
-                    mxu(high, ql[depth, cols], NN) + mxu(low, qh[depth, cols], NN)
+                change = mxu(high, qh[0, :, cols], NN) + (
+                    mxu(high, ql[0, :, cols], NN) + mxu(low, qh[0, :, cols], NN)
                 )
                 for k in range(block_rows // NB):
                     for j in range(2):
                         spot = pl.ds((at + k * NB) * tiles + b + j, NB, stride=tiles)
                         part = change[k * NB : (k + 1) * NB, j * NB : (j + 1) * NB]
                         abuf[spot, :] = abuf[spot, :] - part
-            if finish:
-                area = pl.ds(pl.multiple_of(at * tiles, block_rows), block_rows * tiles)
-                pltpu.make_async_copy(abuf.at[area], out_hbm.at[area], osem).start()
             return carry
 
         lax.fori_loop(0, rows // block_rows, one, 0)
@@ -392,16 +402,15 @@
         sum_start(0, [dot3(mine, mine, TN), first, second], 9, over_cols, c)
 
     t_ref[...] = zero_tile
+    g_mine = (0, pl.ds(0, 3), pl.ds(c * pc, pc))
+
+    @pl.when(r == 0)
+    def _():
+        ar_res[0, 0:3, pl.ds(c * pc, pc), :] = sum_slots(0, 3, 9)
+        over_rows(19, lambda j: ar_res.at[g_mine], lambda j: ar_res.at[g_mine])
+
     scatter_wait(0)
     gather_rows_start(xc.at[0], 6)
-
-    g_mine = (0, pl.ds(0, 3), pl.ds(c * pc, pc))
-
-    @pl.when(r == 0)
-    def _():
-        ar_res[0, 0:3, pl.ds(c * pc, pc), :] = sum_slots(0, 3, 9)
-        over_rows(19, lambda j: ar_res.at[g_mine], lambda j: ar_res.at[g_mine])
-
     gather_cols_start(xr.at[0], 8)
 
     def to_parts(a, carry):
@@ -414,19 +423,6 @@
 
     lax.fori_loop(0, tiles, to_parts, 0)
 
-    @pl.when(r == 0)
-    def _():
-        wait_sent(19, ar_res.at[0, pl.ds(0, 3), pl.ds(0, (n - 1) * pc)])
-
-    @pl.when(r != 0)
-    def _():
-        wait_received(19, ar_res.at[g_mine])
-
-    sum_spread(0, 3, 9, over_cols, c)
-    scatter_wait(1)
-    gather_cols_start(xr.at[1], 13)
-    scatter_wait(2)
-
     def to_flipped(b, carry):
         at = pl.multiple_of(b * NB, NB)
         for a in range(tiles):
@@ -435,8 +431,21 @@
             tlo[pl.ds(at, NB), a * NB : (a + 1) * NB] = low
         return carry
 
-    lax.fori_loop(0, tiles, to_flipped, 0)
+    lax.fori_loop(0, tiles // 2, to_flipped, 0)
+
+    @pl.when(r == 0)
+    def _():
+        wait_sent(19, ar_res.at[0, pl.ds(0, 3), pl.ds(0, (n - 1) * pc)])
+
+    @pl.when(r != 0)
+    def _():
+        wait_received(19, ar_res.at[g_mine])
+
+    sum_spread(0, 3, 9, over_cols, c)
+    scatter_wait(1)
+    scatter_wait(2)
     gather_rows_mid(xc.at[0], 6)
+    gather_cols_start(xr.at[1], 13)
     gather_rows_wait(xc.at[0], 6)
 
     both = halves(flat(xc.at[0]))
@@ -456,21 +465,19 @@
 
     lax.fori_loop(0, tiles, first_product, 0)
     wslot_r[c] = wpart_r[pl.ds(c * ch, ch), :]
-    gather_rows_start(xc.at[1], 11)
     gather_cols_wait(xr.at[0], 8)
     all_start(0, dot3(xr[0], wpart_r[...], TN), 26, over_rows, r)
+    gather_rows_start(xc.at[1], 11)
+    sum_wait(0, 3, 9)
+    g_ref[...] = ar_res[0, 0]
+    cholesky_blocks(g_ref, r0_ref, 0, CHOL_BLOCKS)
     gather_cols_wait(xr.at[1], 13)
     first = jnp.where(r == 1, xr[1, 0:NB], 0.0)
     second = jnp.where(r == 2, xr[1, 0:NB], 0.0)
     sum_start(1, [dot3(xr[0], xr[1], TN), first, second], 14, over_rows, r)
-    sum_wait(0, 3, 9)
-    g_ref[...] = ar_res[0, 0]
-    cholesky_blocks(g_ref, r0_ref, 0, NB // 16)
     all_mid(0, 26, over_cols, c)
-    sum_mid(1, 3, 14, over_rows, r)
-    gather_rows_mid(xc.at[1], 11)
-    gather_rows_start(xc.at[2], 16)
-    cholesky_blocks(g_ref, r0_ref, NB // 16, NB // 8)
+    y_ref[...] = ar_res[0, 0] + exact(ar_res[0, 1], r0_ref[...], TN)
+    inverse_blocks(y_ref, t_ref, 0, INV_BLOCKS // 2)
 
     wait(20, wslot_r.at[pl.ds(0, n - 1)])
     total = wslot_r[0]
@@ -488,11 +495,12 @@
     def _():
         wc[0, level, parity] = total
 
+    sum_mid(1, 3, 14, over_rows, r)
     all_late(0, 26, over_rows, r)
-    y_ref[...] = ar_res[0, 0] + exact(ar_res[0, 1], r0_ref[...], TN)
-    inverse_blocks(y_ref, t_ref, 0, 3 * NB // 32)
-    sum_wait(1, 3, 14)
-    gather_rows_mid(xc.at[2], 16)
+    gather_rows_mid(xc.at[1], 11)
+    gather_rows_start(xc.at[2], 16)
+    inverse_blocks(y_ref, t_ref, INV_BLOCKS // 2, INV_BLOCKS)
+    lax.fori_loop(tiles // 2, tiles, to_flipped, 0)
 
     @pl.when(r != c)
     def _():
@@ -500,18 +508,24 @@
         wait_sent(22, wch.at[0])
 
     gather_rows_start(wc.at[0], 24)
-    inverse_blocks(y_ref, t_ref, 3 * NB // 32, NB // 8)
+    sum_wait(1, 3, 14)
     r0 = r0_ref[...]
     z0 = y_ref[...]
     k0 = ar_res[1, 0]
     rz0 = exact(r0, z0)
     f01 = ar_res[0, 1] + r0
     f02 = ar_res[0, 2]
+    known = known_part(r0, k0, ar_res[1, 1])
+    c01 = exact(k0, z0, TN) + exact(ar_res[1, 1], rz0)
     all_wait(0, 26)
-    b0 = core(r0, z0, h_res[0], k0, ar_res[1, 1])
-    c01 = exact(k0, z0, TN) + exact(ar_res[1, 1], rz0) - exact(f01, b0)
+    b0 = core(z0, h_res[0] + known)
+    c01 = c01 - exact(f01, b0)
     coef = jnp.concatenate([z0, rz0, -b0], axis=0)
-    back = jnp.concatenate([f01, c01], axis=1)
+    carried = exact(coef, f01, NT)
+    last = carried[2 * NB :] + c01.T
+    coef = jnp.concatenate(
+        [coef, jnp.concatenate([carried[: 2 * NB], last], axis=0)], axis=1
+    )
 
     def first_panel(f_ref, c_ref, x0, x1, w, index):
         f_ref[0] = x0
@@ -520,14 +534,13 @@
         def _():
             f_ref[0, 0:NB, :] = f_ref[0, 0:NB, :] + r0
 
-        c_ref[0] = dot3(jnp.concatenate([w, x1, f_ref[0]], axis=1), coef, NN)
+        out = dot3(jnp.concatenate([w, x1, f_ref[0]], axis=1), coef, NN)
+        c_ref[0] = out[:, :NB]
+        f_ref[1] = x1 - out[:, NB:]
 
         @pl.when(index == 0)
         def _():
             c_ref[0, 0:NB, :] = zero_tile
-
-        left = jnp.concatenate([c_ref[0], f_ref[0]], axis=1)
-        f_ref[1] = x1 - dot3(left, back, NT)
 
         @pl.when(index <= 1)
         def _():
@@ -539,8 +552,8 @@
 
     p1r = panel_r[1]
     first = jnp.where(r == 2, p1r[0:NB], 0.0)
-    inner = dot3(jnp.concatenate([p1r, panel_r[0], cor_r[0]], axis=1), p1r, TN)
-    sum_start(2, [inner[0:NB], inner[NB : 2 * NB], inner[2 * NB :], first], 30, over_rows, r)
+    inner = dot3(p1r, jnp.concatenate([p1r, panel_r[0], cor_r[0]], axis=1), TN)
+    sum_start(2, [inner[:, 0:NB], inner[:, NB : 2 * NB], inner[:, 2 * NB :], first], 30, over_rows, r)
     both = halves(p1r)
 
     def second_product(b, carry):
@@ -553,7 +566,6 @@
 
     lax.fori_loop(0, tiles, second_product, 0)
     send(wpart_c.at[:, 1 - parity], wsib, 34, sibling)
-    gather_rows_mid(wc.at[0], 24)
     sum_mid(2, 4, 30, over_rows, r)
     wait(34, wsib)
     wsum[...] = wpart_c[:, parity] + wsib[...]
@@ -565,6 +577,8 @@
 
     lax.fori_loop(1, half, spread, 0)
     wslot_c[level] = wsum[level]
+    gather_rows_mid(xc.at[2], 16)
+    gather_rows_mid(wc.at[0], 24)
     gather_rows_wait(xc.at[1], 11)
     gather_rows_wait(xc.at[2], 16)
     gather_rows_wait(wc.at[0], 24)
@@ -573,15 +587,12 @@
     all_start(1, dot3(p1c, flat(wpart_c), TN), 36, over_cols, c)
     x2c = flat(xc.at[2])
     first = jnp.where(c == 2, x2c[0:NB], 0.0)
-    inner = dot3(jnp.concatenate([flat(xc.at[0]), p1c], axis=1), x2c, TN)
-    sum_start(3, [inner[0:NB], inner[NB:], first], 32, over_cols, c)
-    keep_left(0, cor_r[0])
-    keep_left(1, panel_r[0])
-    keep_right(0, panel_c[0])
-    keep_right(1, cor_c[0])
+    inner = dot3(x2c, jnp.concatenate([flat(xc.at[0]), p1c], axis=1), TN)
+    sum_start(3, [inner[:, 0:NB], inner[:, NB:], first], 32, over_cols, c)
     sum_wait(2, 4, 30)
     g_ref[...] = ar_res[2, 0]
-    cholesky_blocks(g_ref, r1_ref, 0, NB // 16)
+    cholesky_blocks(g_ref, r1_ref, 0, CHOL_BLOCKS)
+    all_mid(1, 36, over_rows, r)
 
     wait(35, wslot_c.at[pl.ds(0, half - 1)])
     total = wslot_c[0]
@@ -599,11 +610,11 @@
     def _():
         wr[1, pl.ds(c * ch, ch), :] = total
 
-    all_mid(1, 36, over_rows, r)
     sum_mid(3, 3, 32, over_cols, c)
-    cholesky_blocks(g_ref, r1_ref, NB // 16, NB // 8)
+    y_ref[...] = ar_res[2, 0] + exact(ar_res[2, 3], r1_ref[...], TN)
+    inverse_blocks(y_ref, t_ref, 0, INV_BLOCKS // 2)
     all_late(1, 36, over_cols, c)
-    y_ref[...] = ar_res[2, 0] + exact(ar_res[2, 3], r1_ref[...], TN)
+    inverse_blocks(y_ref, t_ref, INV_BLOCKS // 2, INV_BLOCKS)
 
     @pl.when(r != c)
     def _():
@@ -611,26 +622,28 @@
         wait_sent(41, wch.at[1])
 
     gather_cols_start(wr.at[1], 42)
-    inverse_blocks(y_ref, t_ref, 0, NB // 16)
-    gather_rows_mid(wc.at[1], 39)
-    inverse_blocks(y_ref, t_ref, NB // 16, NB // 8)
-    apply(0, False)
+    keep_left(0, cor_r[0], panel_r[0])
+    keep_right(0, panel_c[0], cor_c[0])
+    apply_first()
     write_band(0, r0_ref)
     write_band(1, r1_ref)
+    pltpu.make_async_copy(abuf, a_out, asem).start()
+    gather_rows_mid(wc.at[1], 39)
     r1 = r1_ref[...]
     z1 = y_ref[...]
-    j1 = ar_res[2, 1]
-    j2 = ar_res[2, 2]
+    j1t = ar_res[2, 1]
+    j2t = ar_res[2, 2]
     rz1 = exact(r1, z1)
     sum_wait(3, 3, 32)
-    c02 = exact(ar_res[3, 0], z0, TN) + exact(ar_res[1, 2], rz0) - exact(f02, b0)
-    cross = exact(j2, j1, TN)
+    c02 = exact(ar_res[3, 0], z0) + exact(ar_res[1, 2], rz0) - exact(f02, b0)
+    cross = exact(j2t, j1t, NT)
     cf = exact(c02, f02, NT)
-    k1 = ar_res[3, 1] - exact(j2, f02, TT) - exact(j1, c02, TT)
-    fold1 = -exact(j1, z1) - exact(f02, rz1, TN)
-    fold2 = -exact(j2, z1) - exact(c02, rz1, TN)
+    k1 = ar_res[3, 1].T - exact(j2t, f02, NT) - exact(j1t, c02, NT)
+    known = known_part(r1, k1, ar_res[3, 2] - cf - cf.T) - cross - cross.T
+    fold1 = -exact(j1t, z1, TN) - exact(f02, rz1, TN)
+    fold2 = -exact(j2t, z1, TN) - exact(c02, rz1, TN)
     all_wait(1, 36)
-    b1 = core(r1, z1, h_res[1] - cross - cross.T, k1, ar_res[3, 2] - cf - cf.T)
+    b1 = core(z1, h_res[1] + known)
     coef = jnp.concatenate([z1, rz1, fold1, fold2, -b1], axis=0)
 
     def second_panel(f_ref, c_ref, x2, w, index):
@@ -646,15 +659,37 @@
 
     gather_rows_wait(wc.at[1], 39)
     second_panel(panel_c, cor_c, flat(xc.at[2]), flat(wc.at[1]), c)
-    keep_right(2, panel_c[1])
-    keep_right(3, cor_c[1])
+    keep_right(1, panel_c[1], cor_c[1])
+    pltpu.make_async_copy(qh.at[1], qh_out, osem).start()
+    pltpu.make_async_copy(ql.at[1], ql_out, osem2).start()
     gather_cols_wait(xr.at[2], 18)
     gather_cols_wait(wr.at[1], 42)
     second_panel(panel_r, cor_r, xr[2], wr[1], r)
-    keep_left(2, cor_r[1])
-    keep_left(3, panel_r[1])
-    apply(1, True)
-    pltpu.make_async_copy(abuf, out_hbm, osem).wait()
+    keep_left(1, cor_r[1], panel_r[1])
+    last_high = pltpu.make_async_copy(lh.at[1], lh_out, osem3)
+    last_low = pltpu.make_async_copy(ll.at[1], ll_out, osem4)
+    last_high.start()
+    last_low.start()
+    pltpu.make_async_copy(abuf, a_out, asem).wait()
+    pltpu.make_async_copy(qh.at[1], qh_out, osem).wait()
+    pltpu.make_async_copy(ql.at[1], ql_out, osem2).wait()
+    last_high.wait()
+    last_low.wait()
+
+
+def update_kernel(tiles, a_ref, lh, ll, qh, ql, o_ref):
+    high = lh[...]
+    low = ll[...]
+    for b in range(0, tiles, 2):
+        cols = slice(b * NB, (b + 2) * NB)
+        change = mxu(high, qh[:, cols], NN) + (
+            mxu(high, ql[:, cols], NN) + mxu(low, qh[:, cols], NN)
+        )
+        for k in range(high.shape[0] // NB):
+            for j in range(2):
+                spot = pl.ds(k * NB * tiles + b + j, NB, stride=tiles)
+                part = change[k * NB : (k + 1) * NB, j * NB : (j + 1) * NB]
+                o_ref[spot, :] = a_ref[spot, :] - part
 
 
 def local(hamiltonian):
@@ -690,10 +725,10 @@
         ((2, rows, NB), f32),
         ((2, rows, NB), f32),
         ((2, rows, NB), f32),
-        ((rows, 4 * NB), bf16),
-        ((rows, 4 * NB), bf16),
-        ((4 * NB, rows), bf16),
-        ((4 * NB, rows), bf16),
+        ((2, rows, 2 * NB), bf16),
+        ((2, rows, 2 * NB), bf16),
+        ((2, 2 * NB, rows), bf16),
+        ((2, 2 * NB, rows), bf16),
         ((4, 4, NB, NB), f32),
         ((4, n, 4, pc, NB), f32),
         ((4, 4, NB, NB), f32),
@@ -703,23 +738,35 @@
         ((2, n, pc, NB), f32),
         ((2, NB, NB), f32),
     ] + [((NB, NB), f32)] * 5
-    result = pl.pallas_call(
+    anywhere = pl.BlockSpec(memory_space=pl.ANY)
+    left = jax.ShapeDtypeStruct((rows, 2 * NB), bf16)
+    right = jax.ShapeDtypeStruct((2 * NB, rows), bf16)
+    parts = pl.pallas_call(
         functools.partial(reduce_kernel, n, tiles),
-        out_shape=jax.ShapeDtypeStruct((rows * tiles, NB), f32),
-        in_specs=[pl.BlockSpec(memory_space=pl.ANY)],
-        out_specs=pl.BlockSpec(memory_space=pl.ANY),
+        out_shape=[jax.ShapeDtypeStruct((rows * tiles, NB), f32), left, left, right, right],
+        in_specs=[anywhere],
+        out_specs=[anywhere] * 5,
         scratch_shapes=[pltpu.VMEM(*shape) for shape in shapes]
-        + [
-            pltpu.SemaphoreType.DMA,
-            pltpu.SemaphoreType.DMA,
-            pltpu.SemaphoreType.DMA((43,)),
-            pltpu.SemaphoreType.DMA((43,)),
-        ],
+        + [pltpu.SemaphoreType.DMA] * 5
+        + [pltpu.SemaphoreType.DMA((43,))] * 2,
         compiler_params=pltpu.CompilerParams(
             collective_id=0, has_side_effects=True, vmem_limit_bytes=VMEM_LIMIT
         ),
         name="reduce_panels",
     )(block)
+    step = min(rows, 2 * NB)
+    block_spec = pl.BlockSpec((step * tiles, NB), lambda i: (i, 0))
+    left_spec = pl.BlockSpec((step, 2 * NB), lambda i: (i, 0))
+    right_spec = pl.BlockSpec((2 * NB, rows), lambda i: (0, 0))
+    result = pl.pallas_call(
+        functools.partial(update_kernel, tiles),
+        out_shape=jax.ShapeDtypeStruct((rows * tiles, NB), f32),
+        grid=(rows // step,),
+        in_specs=[block_spec, left_spec, left_spec, right_spec, right_spec],
+        out_specs=block_spec,
+        compiler_params=pltpu.CompilerParams(vmem_limit_bytes=VMEM_LIMIT),
+        name="update_matrix",
+    )(*parts)
     return result.reshape(hamiltonian.shape)
 
 

time: 135 us -> 120 us (0.89); the launches traced: 135 us -> 119 us
  Pallas kernels: 128 us -> 119 us
  local copies, waits for them, and re-layouts: 7.08 us -> 0 us
    pallas_call x1 -> x2, Pallas kernels: 128 us -> 119 us  [the longest x1 112 us: local(): pl.pallas_call(functools.partial(reduce_kernel, n, tiles), out_shape=[jax...]
    unnamed x1 -> x0, local copies, waits for them, and re-layouts: 7.08 us -> none
where the time goes in v3:
time: 120 us; the launch traced here: 119 us
  Pallas kernels  119 us (99%)
    pallas_call x1, Pallas kernels, local(): pl.pallas_call(functools.partial(reduce_kernel, n, tiles), out_shape=[jax...  112 us
    pallas_call x1, Pallas kernels, local(): pl.pallas_call(functools.partial(update_kernel, tiles), out_shape=jax.Sha...  6.67 us

profile of v3, /device:TPU:1, one launch (start us, length us, event | category | flops | bytes accessed | tf_op | source)
XLA Modules:
  0.0 118.8 jit_solution(15175616497347905394)
XLA Ops:
  0.0 112.2 %reduce_panels.1 = (f32[8192,128]{1,0:T(8,128)}, bf16[1024,256]{1,0:T(8,128)(2,1)}, bf16[1024,256]{1,0:T(8,128)(2,1)}, bf16[256,1024]{1,0:T(8,128)(2,1)}, bf16[256,1024]{1,0:T(8,128)(2,1)}) custom-call(f32[8192,128]{1,0:T(8,128)} %bitcast.4), custom_call_target="tpu_custom_call" | custom-call | tf_op jit(solution)/shard_map/reduce_panels/pallas_call | solution.py:744
  112.2 6.7 %update_matrix.1 = f32[8192,128]{1,0:T(8,128)} custom-call(f32[8192,128]{1,0:T(8,128)} %get-tuple-element.10.a_ref, bf16[1024,256]{1,0:T(8,128)(2,1)} %get-tuple-element.11.lh, bf16[1024,256]{1,0:T(8,128)(2,1)} %get-tuple-element.12.ll, bf16[256,1024]{1,0:T(8,128)(2,1)} %get-tuple-element.13.qh, bf16[256,1024]{1,0:T(8,128)(2,1)} %get-tuple-element.14.ql), custom_call_target="tpu_custom_call" | custom-call | tf_op jit(solution)/shard_map/update_matrix/pallas_call | solution.py:761

commit v4 on v3

--- a/solution.py
+++ b/solution.py
@@ -391,8 +391,42 @@
                 stg_c[0:NB, :] = zero_tile
 
     pl.semaphore_wait(barrier, 2 * (n - 1) + jnp.where(r != c, 1, 0))
-    for t in range(3):
-        scatter(t)
+    scatter(0)
+
+    def tile_start(sem, index, t, owner):
+        @pl.when((r == t) & (c == owner))
+        def _():
+            over_cols(
+                sem,
+                lambda j: stg_c.at[pl.ds(j * pc, pc)],
+                lambda j: ar_res.at[0, index, pl.ds(j * pc, pc)],
+            )
+            ar_res[0, index, pl.ds(c * pc, pc), :] = stg_c[pl.ds(c * pc, pc), :]
+
+    def tile_wait(sem, index, t, owner):
+        @pl.when((r == t) & (c == owner))
+        def _():
+            wait_sent(sem, stg_c.at[pl.ds(0, (n - 1) * pc)])
+
+        @pl.when((r == t) & (c != owner))
+        def _():
+            wait_received(sem, ar_res.at[0, index, pl.ds(c * pc, pc)])
+
+    def row_start(sem, t, first, count):
+        mine = (0, pl.ds(first, count), pl.ds(c * pc, pc))
+
+        @pl.when(r == t)
+        def _():
+            over_rows(sem, lambda j: ar_res.at[mine], lambda j: ar_res.at[mine])
+
+    def row_wait(sem, t, first, count):
+        @pl.when(r == t)
+        def _():
+            wait_sent(sem, ar_res.at[0, pl.ds(first, count), pl.ds(0, (n - 1) * pc)])
+
+        @pl.when(r != t)
+        def _():
+            wait_received(sem, ar_res.at[0, pl.ds(first, count), pl.ds(c * pc, pc)])
 
     @pl.when(r == 0)
     def _():
@@ -402,16 +436,20 @@
         sum_start(0, [dot3(mine, mine, TN), first, second], 9, over_cols, c)
 
     t_ref[...] = zero_tile
-    g_mine = (0, pl.ds(0, 3), pl.ds(c * pc, pc))
 
     @pl.when(r == 0)
     def _():
         ar_res[0, 0:3, pl.ds(c * pc, pc), :] = sum_slots(0, 3, 9)
-        over_rows(19, lambda j: ar_res.at[g_mine], lambda j: ar_res.at[g_mine])
-
+
+    row_start(19, 0, 0, 3)
     scatter_wait(0)
     gather_rows_start(xc.at[0], 6)
     gather_cols_start(xr.at[0], 8)
+    scatter(1)
+    tile_start(43, 3, 1, 1)
+    tile_start(44, 4, 1, 2)
+    scatter(2)
+    tile_start(45, 5, 2, 2)
 
     def to_parts(a, carry):
         at = pl.multiple_of(a * NB, NB)
@@ -433,19 +471,17 @@
 
     lax.fori_loop(0, tiles // 2, to_flipped, 0)
 
-    @pl.when(r == 0)
-    def _():
-        wait_sent(19, ar_res.at[0, pl.ds(0, 3), pl.ds(0, (n - 1) * pc)])
-
-    @pl.when(r != 0)
-    def _():
-        wait_received(19, ar_res.at[g_mine])
-
+    row_wait(19, 0, 0, 3)
     sum_spread(0, 3, 9, over_cols, c)
+    tile_wait(43, 3, 1, 1)
+    tile_wait(44, 4, 1, 2)
+    tile_wait(45, 5, 2, 2)
+    row_start(46, 1, 3, 2)
+    row_start(47, 2, 5, 1)
     scatter_wait(1)
+    gather_cols_start(xr.at[1], 13)
     scatter_wait(2)
     gather_rows_mid(xc.at[0], 6)
-    gather_cols_start(xr.at[1], 13)
     gather_rows_wait(xc.at[0], 6)
 
     both = halves(flat(xc.at[0]))
@@ -468,14 +504,14 @@
     gather_cols_wait(xr.at[0], 8)
     all_start(0, dot3(xr[0], wpart_r[...], TN), 26, over_rows, r)
     gather_rows_start(xc.at[1], 11)
+    gather_cols_start(xr.at[2], 18)
     sum_wait(0, 3, 9)
     g_ref[...] = ar_res[0, 0]
     cholesky_blocks(g_ref, r0_ref, 0, CHOL_BLOCKS)
+    all_mid(0, 26, over_cols, c)
     gather_cols_wait(xr.at[1], 13)
-    first = jnp.where(r == 1, xr[1, 0:NB], 0.0)
-    second = jnp.where(r == 2, xr[1, 0:NB], 0.0)
-    sum_start(1, [dot3(xr[0], xr[1], TN), first, second], 14, over_rows, r)
-    all_mid(0, 26, over_cols, c)
+    sum_start(1, [dot3(xr[0], xr[1], TN)], 14, over_rows, r)
+    gather_rows_start(xc.at[2], 16)
     y_ref[...] = ar_res[0, 0] + exact(ar_res[0, 1], r0_ref[...], TN)
     inverse_blocks(y_ref, t_ref, 0, INV_BLOCKS // 2)
 
@@ -484,7 +520,6 @@
     for j in range(1, n):
         total = total + wslot_r[j]
     wr[0, pl.ds(c * ch, ch), :] = total
-    gather_cols_start(wr.at[0], 23)
     wch[0] = total
 
     @pl.when(r != c)
@@ -495,12 +530,16 @@
     def _():
         wc[0, level, parity] = total
 
-    sum_mid(1, 3, 14, over_rows, r)
+    gather_cols_start(wr.at[0], 23)
     all_late(0, 26, over_rows, r)
-    gather_rows_mid(xc.at[1], 11)
-    gather_rows_start(xc.at[2], 16)
+    sum_mid(1, 1, 14, over_rows, r)
+    row_wait(46, 1, 3, 2)
+    row_wait(47, 2, 5, 1)
+    tiles_mine = (0, pl.ds(3, 3), pl.ds(c * pc, pc))
+    over_cols(48, lambda j: ar_res.at[tiles_mine], lambda j: ar_res.at[tiles_mine])
     inverse_blocks(y_ref, t_ref, INV_BLOCKS // 2, INV_BLOCKS)
     lax.fori_loop(tiles // 2, tiles, to_flipped, 0)
+    gather_rows_mid(xc.at[1], 11)
 
     @pl.when(r != c)
     def _():
@@ -508,15 +547,19 @@
         wait_sent(22, wch.at[0])
 
     gather_rows_start(wc.at[0], 24)
-    sum_wait(1, 3, 14)
+    wait(48, ar_res.at[0, pl.ds(3, 3), pl.ds(0, (n - 1) * pc)])
+    sum_wait(1, 1, 14)
     r0 = r0_ref[...]
     z0 = y_ref[...]
     k0 = ar_res[1, 0]
     rz0 = exact(r0, z0)
     f01 = ar_res[0, 1] + r0
     f02 = ar_res[0, 2]
-    known = known_part(r0, k0, ar_res[1, 1])
-    c01 = exact(k0, z0, TN) + exact(ar_res[1, 1], rz0)
+    x11 = ar_res[0, 3]
+    x12 = ar_res[0, 4]
+    x22 = ar_res[0, 5]
+    known = known_part(r0, k0, x11)
+    c01 = exact(k0, z0, TN) + exact(x11, rz0)
     all_wait(0, 26)
     b0 = core(z0, h_res[0] + known)
     c01 = c01 - exact(f01, b0)
@@ -547,13 +590,10 @@
             f_ref[1, 0:NB, :] = zero_tile
 
     gather_cols_wait(wr.at[0], 23)
-    gather_cols_start(xr.at[2], 18)
     first_panel(panel_r, cor_r, xr[0], xr[1], wr[0], r)
 
     p1r = panel_r[1]
-    first = jnp.where(r == 2, p1r[0:NB], 0.0)
-    inner = dot3(p1r, jnp.concatenate([p1r, panel_r[0], cor_r[0]], axis=1), TN)
-    sum_start(2, [inner[:, 0:NB], inner[:, NB : 2 * NB], inner[:, 2 * NB :], first], 30, over_rows, r)
+    sum_start(2, [dot3(p1r, p1r, TN)], 30, over_rows, r)
     both = halves(p1r)
 
     def second_product(b, carry):
@@ -566,7 +606,8 @@
 
     lax.fori_loop(0, tiles, second_product, 0)
     send(wpart_c.at[:, 1 - parity], wsib, 34, sibling)
-    sum_mid(2, 4, 30, over_rows, r)
+    gather_cols_wait(xr.at[2], 18)
+    sum_mid(2, 1, 30, over_rows, r)
     wait(34, wsib)
     wsum[...] = wpart_c[:, parity] + wsib[...]
 
@@ -586,20 +627,21 @@
     p1c = panel_c[1]
     all_start(1, dot3(p1c, flat(wpart_c), TN), 36, over_cols, c)
     x2c = flat(xc.at[2])
-    first = jnp.where(c == 2, x2c[0:NB], 0.0)
-    inner = dot3(x2c, jnp.concatenate([flat(xc.at[0]), p1c], axis=1), TN)
-    sum_start(3, [inner[:, 0:NB], inner[:, NB:], first], 32, over_cols, c)
-    sum_wait(2, 4, 30)
+    inner = dot3(p1c, jnp.concatenate([x2c, panel_c[0], cor_c[0]], axis=1), TN)
+    sum_start(3, [inner[:, 0:NB], inner[:, NB : 2 * NB], inner[:, 2 * NB :]], 32, over_cols, c)
+    sum_start(4, [dot3(xr[2], xr[0], TN)], 49, over_rows, r)
+    keep_left(0, cor_r[0], panel_r[0])
+    keep_right(0, panel_c[0], cor_c[0])
+    sum_wait(2, 1, 30)
     g_ref[...] = ar_res[2, 0]
-    cholesky_blocks(g_ref, r1_ref, 0, CHOL_BLOCKS)
+    cholesky_blocks(g_ref, r1_ref, 0, CHOL_BLOCKS // 2)
     all_mid(1, 36, over_rows, r)
+    sum_mid(4, 1, 49, over_rows, r)
 
     wait(35, wslot_c.at[pl.ds(0, half - 1)])
     total = wslot_c[0]
     for j in range(1, half):
         total = total + wslot_c[j]
-    wc[1, level, parity] = total
-    gather_rows_start(wc.at[1], 39)
     wch[1] = total
 
     @pl.when(r != c)
@@ -610,11 +652,16 @@
     def _():
         wr[1, pl.ds(c * ch, ch), :] = total
 
+    wc[1, level, parity] = total
+    gather_rows_start(wc.at[1], 39)
+    cholesky_blocks(g_ref, r1_ref, CHOL_BLOCKS // 2, CHOL_BLOCKS)
     sum_mid(3, 3, 32, over_cols, c)
-    y_ref[...] = ar_res[2, 0] + exact(ar_res[2, 3], r1_ref[...], TN)
+    all_late(1, 36, over_cols, c)
+    sum_wait(4, 1, 49)
+    c02 = exact(ar_res[4, 0], z0) + exact(x12, rz0) - exact(f02, b0)
+    top = x12 - exact(c02, f01, NT) - exact(f02, c01, NT)
+    y_ref[...] = ar_res[2, 0] + exact(top, r1_ref[...], TN)
     inverse_blocks(y_ref, t_ref, 0, INV_BLOCKS // 2)
-    all_late(1, 36, over_cols, c)
-    inverse_blocks(y_ref, t_ref, INV_BLOCKS // 2, INV_BLOCKS)
 
     @pl.when(r != c)
     def _():
@@ -622,26 +669,24 @@
         wait_sent(41, wch.at[1])
 
     gather_cols_start(wr.at[1], 42)
-    keep_left(0, cor_r[0], panel_r[0])
-    keep_right(0, panel_c[0], cor_c[0])
+    inverse_blocks(y_ref, t_ref, INV_BLOCKS // 2, INV_BLOCKS)
+    gather_rows_mid(wc.at[1], 39)
+    r1 = r1_ref[...]
+    z1 = y_ref[...]
+    rz1 = exact(r1, z1)
+    sum_wait(3, 3, 32)
+    j1t = ar_res[3, 1]
+    j2t = ar_res[3, 2]
+    cross = exact(j2t, j1t, NT)
+    cf = exact(c02, f02, NT)
+    k1 = ar_res[3, 0] - exact(j2t, f02, NT) - exact(j1t, c02, NT)
+    known = known_part(r1, k1, x22 - cf - cf.T) - cross - cross.T
+    fold1 = -exact(j1t, z1, TN) - exact(f02, rz1, TN)
+    fold2 = -exact(j2t, z1, TN) - exact(c02, rz1, TN)
     apply_first()
     write_band(0, r0_ref)
     write_band(1, r1_ref)
     pltpu.make_async_copy(abuf, a_out, asem).start()
-    gather_rows_mid(wc.at[1], 39)
-    r1 = r1_ref[...]
-    z1 = y_ref[...]
-    j1t = ar_res[2, 1]
-    j2t = ar_res[2, 2]
-    rz1 = exact(r1, z1)
-    sum_wait(3, 3, 32)
-    c02 = exact(ar_res[3, 0], z0) + exact(ar_res[1, 2], rz0) - exact(f02, b0)
-    cross = exact(j2t, j1t, NT)
-    cf = exact(c02, f02, NT)
-    k1 = ar_res[3, 1].T - exact(j2t, f02, NT) - exact(j1t, c02, NT)
-    known = known_part(r1, k1, ar_res[3, 2] - cf - cf.T) - cross - cross.T
-    fold1 = -exact(j1t, z1, TN) - exact(f02, rz1, TN)
-    fold2 = -exact(j2t, z1, TN) - exact(c02, rz1, TN)
     all_wait(1, 36)
     b1 = core(z1, h_res[1] + known)
     coef = jnp.concatenate([z1, rz1, fold1, fold2, -b1], axis=0)
@@ -662,7 +707,6 @@
     keep_right(1, panel_c[1], cor_c[1])
     pltpu.make_async_copy(qh.at[1], qh_out, osem).start()
     pltpu.make_async_copy(ql.at[1], ql_out, osem2).start()
-    gather_cols_wait(xr.at[2], 18)
     gather_cols_wait(wr.at[1], 42)
     second_panel(panel_r, cor_r, xr[2], wr[1], r)
     keep_left(1, cor_r[1], panel_r[1])
@@ -729,9 +773,9 @@
         ((2, rows, 2 * NB), bf16),
         ((2, 2 * NB, rows), bf16),
         ((2, 2 * NB, rows), bf16),
-        ((4, 4, NB, NB), f32),
-        ((4, n, 4, pc, NB), f32),
-        ((4, 4, NB, NB), f32),
+        ((5, 3, NB, NB), f32),
+        ((5, n, 3, pc, NB), f32),
+        ((5, 6, NB, NB), f32),
         ((2, NB, NB), f32),
         ((2, n, pc, NB), f32),
         ((2, pc, NB), f32),
@@ -748,7 +792,7 @@
         out_specs=[anywhere] * 5,
         scratch_shapes=[pltpu.VMEM(*shape) for shape in shapes]
         + [pltpu.SemaphoreType.DMA] * 5
-        + [pltpu.SemaphoreType.DMA((43,))] * 2,
+        + [pltpu.SemaphoreType.DMA((51,))] * 2,
         compiler_params=pltpu.CompilerParams(
             collective_id=0, has_side_effects=True, vmem_limit_bytes=VMEM_LIMIT
         ),

time: 120 us -> 115 us (0.958)
  Pallas kernels: 119 us -> 115 us
    pallas_call x1, Pallas kernels: 112 us -> 108 us  [local(): pl.pallas_call(functools.partial(reduce_kernel, n, tiles), out_shape=[jax...]
where the time goes in v4:
time: 115 us
  Pallas kernels  115 us (100%)
    pallas_call x1, Pallas kernels, local(): pl.pallas_call(functools.partial(reduce_kernel, n, tiles), out_shape=[jax...  108 us
    pallas_call x1, Pallas kernels, local(): pl.pallas_call(functools.partial(update_kernel, tiles), out_shape=jax.Sha...  6.67 us

profile of v4, /device:TPU:1, one launch (start us, length us, event | category | flops | bytes accessed | tf_op | source)
XLA Modules:
  0.0 114.6 jit_solution(9339507452093492780)
XLA Ops:
  0.0 108.0 %reduce_panels.1 = (f32[8192,128]{1,0:T(8,128)}, bf16[1024,256]{1,0:T(8,128)(2,1)}, bf16[1024,256]{1,0:T(8,128)(2,1)}, bf16[256,1024]{1,0:T(8,128)(2,1)}, bf16[256,1024]{1,0:T(8,128)(2,1)}) custom-call(f32[8192,128]{1,0:T(8,128)} %bitcast.4), custom_call_target="tpu_custom_call" | custom-call | tf_op jit(solution)/shard_map/reduce_panels/pallas_call | solution.py:788
  108.0 6.7 %update_matrix.1 = f32[8192,128]{1,0:T(8,128)} custom-call(f32[8192,128]{1,0:T(8,128)} %get-tuple-element.10.a_ref, bf16[1024,256]{1,0:T(8,128)(2,1)} %get-tuple-element.11.lh, bf16[1024,256]{1,0:T(8,128)(2,1)} %get-tuple-element.12.ll, bf16[256,1024]{1,0:T(8,128)(2,1)} %get-tuple-element.13.qh, bf16[256,1024]{1,0:T(8,128)(2,1)} %get-tuple-element.14.ql), custom_call_target="tpu_custom_call" | custom-call | tf_op jit(solution)/shard_map/update_matrix/pallas_call | solution.py:805

commit v5 on v4

--- a/solution.py
+++ b/solution.py
@@ -473,15 +473,15 @@
 
     row_wait(19, 0, 0, 3)
     sum_spread(0, 3, 9, over_cols, c)
+    scatter_wait(1)
+    gather_cols_start(xr.at[1], 13)
+    gather_rows_mid(xc.at[0], 6)
     tile_wait(43, 3, 1, 1)
     tile_wait(44, 4, 1, 2)
     tile_wait(45, 5, 2, 2)
     row_start(46, 1, 3, 2)
     row_start(47, 2, 5, 1)
-    scatter_wait(1)
-    gather_cols_start(xr.at[1], 13)
     scatter_wait(2)
-    gather_rows_mid(xc.at[0], 6)
     gather_rows_wait(xc.at[0], 6)
 
     both = halves(flat(xc.at[0]))
@@ -504,14 +504,12 @@
     gather_cols_wait(xr.at[0], 8)
     all_start(0, dot3(xr[0], wpart_r[...], TN), 26, over_rows, r)
     gather_rows_start(xc.at[1], 11)
-    gather_cols_start(xr.at[2], 18)
     sum_wait(0, 3, 9)
     g_ref[...] = ar_res[0, 0]
     cholesky_blocks(g_ref, r0_ref, 0, CHOL_BLOCKS)
     all_mid(0, 26, over_cols, c)
     gather_cols_wait(xr.at[1], 13)
     sum_start(1, [dot3(xr[0], xr[1], TN)], 14, over_rows, r)
-    gather_rows_start(xc.at[2], 16)
     y_ref[...] = ar_res[0, 0] + exact(ar_res[0, 1], r0_ref[...], TN)
     inverse_blocks(y_ref, t_ref, 0, INV_BLOCKS // 2)
 
@@ -520,6 +518,7 @@
     for j in range(1, n):
         total = total + wslot_r[j]
     wr[0, pl.ds(c * ch, ch), :] = total
+    gather_cols_start(wr.at[0], 23)
     wch[0] = total
 
     @pl.when(r != c)
@@ -530,7 +529,6 @@
     def _():
         wc[0, level, parity] = total
 
-    gather_cols_start(wr.at[0], 23)
     all_late(0, 26, over_rows, r)
     sum_mid(1, 1, 14, over_rows, r)
     row_wait(46, 1, 3, 2)
@@ -570,17 +568,22 @@
         [coef, jnp.concatenate([carried[: 2 * NB], last], axis=0)], axis=1
     )
 
-    def first_panel(f_ref, c_ref, x0, x1, w, index):
+    def first_panel(f_ref, c_ref, x0, x1, index):
         f_ref[0] = x0
 
         @pl.when(index == 1)
         def _():
             f_ref[0, 0:NB, :] = f_ref[0, 0:NB, :] + r0
 
-        out = dot3(jnp.concatenate([w, x1, f_ref[0]], axis=1), coef, NN)
+        out = dot3(jnp.concatenate([x1, f_ref[0]], axis=1), coef[NB:], NN)
         c_ref[0] = out[:, :NB]
         f_ref[1] = x1 - out[:, NB:]
 
+    def first_panel_product(f_ref, c_ref, w, index):
+        out = dot3(w, coef[:NB], NN)
+        c_ref[0] = c_ref[0] + out[:, :NB]
+        f_ref[1] = f_ref[1] - out[:, NB:]
+
         @pl.when(index == 0)
         def _():
             c_ref[0, 0:NB, :] = zero_tile
@@ -589,8 +592,10 @@
         def _():
             f_ref[1, 0:NB, :] = zero_tile
 
+    first_panel(panel_r, cor_r, xr[0], xr[1], r)
     gather_cols_wait(wr.at[0], 23)
-    first_panel(panel_r, cor_r, xr[0], xr[1], wr[0], r)
+    gather_cols_start(xr.at[2], 18)
+    first_panel_product(panel_r, cor_r, wr[0], r)
 
     p1r = panel_r[1]
     sum_start(2, [dot3(p1r, p1r, TN)], 30, over_rows, r)
@@ -606,7 +611,6 @@
 
     lax.fori_loop(0, tiles, second_product, 0)
     send(wpart_c.at[:, 1 - parity], wsib, 34, sibling)
-    gather_cols_wait(xr.at[2], 18)
     sum_mid(2, 1, 30, over_rows, r)
     wait(34, wsib)
     wsum[...] = wpart_c[:, parity] + wsib[...]
@@ -618,25 +622,26 @@
 
     lax.fori_loop(1, half, spread, 0)
     wslot_c[level] = wsum[level]
-    gather_rows_mid(xc.at[2], 16)
     gather_rows_mid(wc.at[0], 24)
+    gather_rows_start(xc.at[2], 16)
     gather_rows_wait(xc.at[1], 11)
-    gather_rows_wait(xc.at[2], 16)
+    first_panel(panel_c, cor_c, flat(xc.at[0]), flat(xc.at[1]), c)
+    gather_cols_wait(xr.at[2], 18)
+    inner = dot3(xr[2], jnp.concatenate([xr[0], panel_r[1]], axis=1), TN)
+    sum_start(4, [inner[:, 0:NB], inner[:, NB:]], 49, over_rows, r)
     gather_rows_wait(wc.at[0], 24)
-    first_panel(panel_c, cor_c, flat(xc.at[0]), flat(xc.at[1]), flat(wc.at[0]), c)
+    first_panel_product(panel_c, cor_c, flat(wc.at[0]), c)
     p1c = panel_c[1]
     all_start(1, dot3(p1c, flat(wpart_c), TN), 36, over_cols, c)
-    x2c = flat(xc.at[2])
-    inner = dot3(p1c, jnp.concatenate([x2c, panel_c[0], cor_c[0]], axis=1), TN)
-    sum_start(3, [inner[:, 0:NB], inner[:, NB : 2 * NB], inner[:, 2 * NB :]], 32, over_cols, c)
-    sum_start(4, [dot3(xr[2], xr[0], TN)], 49, over_rows, r)
+    inner = dot3(p1c, jnp.concatenate([panel_c[0], cor_c[0]], axis=1), TN)
+    sum_start(3, [inner[:, 0:NB], inner[:, NB:]], 32, over_cols, c)
     keep_left(0, cor_r[0], panel_r[0])
     keep_right(0, panel_c[0], cor_c[0])
     sum_wait(2, 1, 30)
     g_ref[...] = ar_res[2, 0]
     cholesky_blocks(g_ref, r1_ref, 0, CHOL_BLOCKS // 2)
     all_mid(1, 36, over_rows, r)
-    sum_mid(4, 1, 49, over_rows, r)
+    sum_mid(4, 2, 49, over_rows, r)
 
     wait(35, wslot_c.at[pl.ds(0, half - 1)])
     total = wslot_c[0]
@@ -655,9 +660,10 @@
     wc[1, level, parity] = total
     gather_rows_start(wc.at[1], 39)
     cholesky_blocks(g_ref, r1_ref, CHOL_BLOCKS // 2, CHOL_BLOCKS)
-    sum_mid(3, 3, 32, over_cols, c)
+    sum_mid(3, 2, 32, over_cols, c)
+    gather_rows_mid(xc.at[2], 16)
     all_late(1, 36, over_cols, c)
-    sum_wait(4, 1, 49)
+    sum_wait(4, 2, 49)
     c02 = exact(ar_res[4, 0], z0) + exact(x12, rz0) - exact(f02, b0)
     top = x12 - exact(c02, f01, NT) - exact(f02, c01, NT)
     y_ref[...] = ar_res[2, 0] + exact(top, r1_ref[...], TN)
@@ -674,12 +680,12 @@
     r1 = r1_ref[...]
     z1 = y_ref[...]
     rz1 = exact(r1, z1)
-    sum_wait(3, 3, 32)
-    j1t = ar_res[3, 1]
-    j2t = ar_res[3, 2]
+    sum_wait(3, 2, 32)
+    j1t = ar_res[3, 0]
+    j2t = ar_res[3, 1]
     cross = exact(j2t, j1t, NT)
     cf = exact(c02, f02, NT)
-    k1 = ar_res[3, 0] - exact(j2t, f02, NT) - exact(j1t, c02, NT)
+    k1 = ar_res[4, 1].T - exact(j2t, f02, NT) - exact(j1t, c02, NT)
     known = known_part(r1, k1, x22 - cf - cf.T) - cross - cross.T
     fold1 = -exact(j1t, z1, TN) - exact(f02, rz1, TN)
     fold2 = -exact(j2t, z1, TN) - exact(c02, rz1, TN)
@@ -691,24 +697,32 @@
     b1 = core(z1, h_res[1] + known)
     coef = jnp.concatenate([z1, rz1, fold1, fold2, -b1], axis=0)
 
-    def second_panel(f_ref, c_ref, x2, w, index):
+    def second_panel(f_ref, c_ref, x2, index):
         @pl.when(index == 2)
         def _():
             f_ref[1, 0:NB, :] = f_ref[1, 0:NB, :] + r1
 
-        c_ref[1] = dot3(jnp.concatenate([w, x2, c_ref[0], f_ref[0], f_ref[1]], axis=1), coef, NN)
+        c_ref[1] = dot3(
+            jnp.concatenate([x2, c_ref[0], f_ref[0], f_ref[1]], axis=1), coef[NB:], NN
+        )
+
+    def second_panel_product(c_ref, w, index):
+        c_ref[1] = c_ref[1] + dot3(w, coef[:NB], NN)
 
         @pl.when(index <= 1)
         def _():
             c_ref[1, 0:NB, :] = zero_tile
 
+    second_panel(panel_r, cor_r, xr[2], r)
+    gather_rows_wait(xc.at[2], 16)
+    second_panel(panel_c, cor_c, flat(xc.at[2]), c)
     gather_rows_wait(wc.at[1], 39)
-    second_panel(panel_c, cor_c, flat(xc.at[2]), flat(wc.at[1]), c)
+    second_panel_product(cor_c, flat(wc.at[1]), c)
     keep_right(1, panel_c[1], cor_c[1])
     pltpu.make_async_copy(qh.at[1], qh_out, osem).start()
     pltpu.make_async_copy(ql.at[1], ql_out, osem2).start()
     gather_cols_wait(wr.at[1], 42)
-    second_panel(panel_r, cor_r, xr[2], wr[1], r)
+    second_panel_product(cor_r, wr[1], r)
     keep_left(1, cor_r[1], panel_r[1])
     last_high = pltpu.make_async_copy(lh.at[1], lh_out, osem3)
     last_low = pltpu.make_async_copy(ll.at[1], ll_out, osem4)

time: 115 us -> 118 us (1.026)
  Pallas kernels: 115 us -> 117 us
    pallas_call x1, Pallas kernels: 108 us -> 111 us  [local(): pl.pallas_call(functools.partial(reduce_kernel, n, tiles), out_shape=[jax...]
where the time goes in v5:
time: 118 us; the launch traced here: 117 us
  Pallas kernels  117 us (99%)
    pallas_call x1, Pallas kernels, local(): pl.pallas_call(functools.partial(reduce_kernel, n, tiles), out_shape=[jax...  111 us
    pallas_call x1, Pallas kernels, local(): pl.pallas_call(functools.partial(update_kernel, tiles), out_shape=jax.Sha...  6.67 us

profile of v5, /device:TPU:1, one launch (start us, length us, event | category | flops | bytes accessed | tf_op | source)
XLA Modules:
  0.0 117.2 jit_solution(4574374172165907606)
XLA Ops:
  0.0 110.5 %reduce_panels.1 = (f32[8192,128]{1,0:T(8,128)}, bf16[1024,256]{1,0:T(8,128)(2,1)}, bf16[1024,256]{1,0:T(8,128)(2,1)}, bf16[256,1024]{1,0:T(8,128)(2,1)}, bf16[256,1024]{1,0:T(8,128)(2,1)}) custom-call(f32[8192,128]{1,0:T(8,128)} %bitcast.4), custom_call_target="tpu_custom_call" | custom-call | tf_op jit(solution)/shard_map/reduce_panels/pallas_call | solution.py:802
  110.5 6.7 %update_matrix.1 = f32[8192,128]{1,0:T(8,128)} custom-call(f32[8192,128]{1,0:T(8,128)} %get-tuple-element.10.a_ref, bf16[1024,256]{1,0:T(8,128)(2,1)} %get-tuple-element.11.lh, bf16[1024,256]{1,0:T(8,128)(2,1)} %get-tuple-element.12.ll, bf16[256,1024]{1,0:T(8,128)(2,1)} %get-tuple-element.13.qh, bf16[256,1024]{1,0:T(8,128)(2,1)} %get-tuple-element.14.ql), custom_call_target="tpu_custom_call" | custom-call | tf_op jit(solution)/shard_map/update_matrix/pallas_call | solution.py:819

commit v6 on v5

--- a/solution.py
+++ b/solution.py
@@ -510,6 +510,7 @@
     all_mid(0, 26, over_cols, c)
     gather_cols_wait(xr.at[1], 13)
     sum_start(1, [dot3(xr[0], xr[1], TN)], 14, over_rows, r)
+    all_start(2, dot3(xr[2, pl.ds(c * ch, ch), :], xr[0, pl.ds(c * ch, ch), :], TN), 49, over_cols, c)
     y_ref[...] = ar_res[0, 0] + exact(ar_res[0, 1], r0_ref[...], TN)
     inverse_blocks(y_ref, t_ref, 0, INV_BLOCKS // 2)
 
@@ -538,6 +539,7 @@
     inverse_blocks(y_ref, t_ref, INV_BLOCKS // 2, INV_BLOCKS)
     lax.fori_loop(tiles // 2, tiles, to_flipped, 0)
     gather_rows_mid(xc.at[1], 11)
+    all_mid(2, 49, over_rows, r)
 
     @pl.when(r != c)
     def _():
@@ -594,7 +596,6 @@
 
     first_panel(panel_r, cor_r, xr[0], xr[1], r)
     gather_cols_wait(wr.at[0], 23)
-    gather_cols_start(xr.at[2], 18)
     first_panel_product(panel_r, cor_r, wr[0], r)
 
     p1r = panel_r[1]
@@ -611,6 +612,7 @@
 
     lax.fori_loop(0, tiles, second_product, 0)
     send(wpart_c.at[:, 1 - parity], wsib, 34, sibling)
+    all_late(2, 49, over_cols, c)
     sum_mid(2, 1, 30, over_rows, r)
     wait(34, wsib)
     wsum[...] = wpart_c[:, parity] + wsib[...]
@@ -623,12 +625,9 @@
     lax.fori_loop(1, half, spread, 0)
     wslot_c[level] = wsum[level]
     gather_rows_mid(wc.at[0], 24)
-    gather_rows_start(xc.at[2], 16)
+    all_start(3, dot3(xr[2, pl.ds(c * ch, ch), :], panel_r[1, pl.ds(c * ch, ch), :], TN), 52, over_cols, c)
     gather_rows_wait(xc.at[1], 11)
     first_panel(panel_c, cor_c, flat(xc.at[0]), flat(xc.at[1]), c)
-    gather_cols_wait(xr.at[2], 18)
-    inner = dot3(xr[2], jnp.concatenate([xr[0], panel_r[1]], axis=1), TN)
-    sum_start(4, [inner[:, 0:NB], inner[:, NB:]], 49, over_rows, r)
     gather_rows_wait(wc.at[0], 24)
     first_panel_product(panel_c, cor_c, flat(wc.at[0]), c)
     p1c = panel_c[1]
@@ -639,14 +638,15 @@
     keep_right(0, panel_c[0], cor_c[0])
     sum_wait(2, 1, 30)
     g_ref[...] = ar_res[2, 0]
-    cholesky_blocks(g_ref, r1_ref, 0, CHOL_BLOCKS // 2)
+    cholesky_blocks(g_ref, r1_ref, 0, CHOL_BLOCKS)
     all_mid(1, 36, over_rows, r)
-    sum_mid(4, 2, 49, over_rows, r)
-
+    all_mid(3, 52, over_rows, r)
+    sum_mid(3, 2, 32, over_cols, c)
     wait(35, wslot_c.at[pl.ds(0, half - 1)])
     total = wslot_c[0]
     for j in range(1, half):
         total = total + wslot_c[j]
+    total = total + exact(xc[2, level, parity], r1_ref[...])
     wch[1] = total
 
     @pl.when(r != c)
@@ -659,12 +659,8 @@
 
     wc[1, level, parity] = total
     gather_rows_start(wc.at[1], 39)
-    cholesky_blocks(g_ref, r1_ref, CHOL_BLOCKS // 2, CHOL_BLOCKS)
-    sum_mid(3, 2, 32, over_cols, c)
-    gather_rows_mid(xc.at[2], 16)
-    all_late(1, 36, over_cols, c)
-    sum_wait(4, 2, 49)
-    c02 = exact(ar_res[4, 0], z0) + exact(x12, rz0) - exact(f02, b0)
+    all_wait(2, 49)
+    c02 = exact(h_res[2], z0) + exact(x12, rz0) - exact(f02, b0)
     top = x12 - exact(c02, f01, NT) - exact(f02, c01, NT)
     y_ref[...] = ar_res[2, 0] + exact(top, r1_ref[...], TN)
     inverse_blocks(y_ref, t_ref, 0, INV_BLOCKS // 2)
@@ -674,6 +670,8 @@
         wait_received(41, wr.at[1, pl.ds(c * ch, ch)])
         wait_sent(41, wch.at[1])
 
+    all_late(1, 36, over_cols, c)
+    all_late(3, 52, over_cols, c)
     gather_cols_start(wr.at[1], 42)
     inverse_blocks(y_ref, t_ref, INV_BLOCKS // 2, INV_BLOCKS)
     gather_rows_mid(wc.at[1], 39)
@@ -681,11 +679,12 @@
     z1 = y_ref[...]
     rz1 = exact(r1, z1)
     sum_wait(3, 2, 32)
+    all_wait(3, 52)
     j1t = ar_res[3, 0]
     j2t = ar_res[3, 1]
     cross = exact(j2t, j1t, NT)
     cf = exact(c02, f02, NT)
-    k1 = ar_res[4, 1].T - exact(j2t, f02, NT) - exact(j1t, c02, NT)
+    k1 = h_res[3].T - exact(j2t, f02, NT) - exact(j1t, c02, NT)
     known = known_part(r1, k1, x22 - cf - cf.T) - cross - cross.T
     fold1 = -exact(j1t, z1, TN) - exact(f02, rz1, TN)
     fold2 = -exact(j2t, z1, TN) - exact(c02, rz1, TN)
@@ -695,15 +694,15 @@
     pltpu.make_async_copy(abuf, a_out, asem).start()
     all_wait(1, 36)
     b1 = core(z1, h_res[1] + known)
-    coef = jnp.concatenate([z1, rz1, fold1, fold2, -b1], axis=0)
-
-    def second_panel(f_ref, c_ref, x2, index):
+    coef = jnp.concatenate([z1, fold1, fold2, -b1], axis=0)
+
+    def second_panel(f_ref, c_ref, index):
         @pl.when(index == 2)
         def _():
             f_ref[1, 0:NB, :] = f_ref[1, 0:NB, :] + r1
 
         c_ref[1] = dot3(
-            jnp.concatenate([x2, c_ref[0], f_ref[0], f_ref[1]], axis=1), coef[NB:], NN
+            jnp.concatenate([c_ref[0], f_ref[0], f_ref[1]], axis=1), coef[NB:], NN
         )
 
     def second_panel_product(c_ref, w, index):
@@ -713,9 +712,8 @@
         def _():
             c_ref[1, 0:NB, :] = zero_tile
 
-    second_panel(panel_r, cor_r, xr[2], r)
-    gather_rows_wait(xc.at[2], 16)
-    second_panel(panel_c, cor_c, flat(xc.at[2]), c)
+    second_panel(panel_r, cor_r, r)
+    second_panel(panel_c, cor_c, c)
     gather_rows_wait(wc.at[1], 39)
     second_panel_product(cor_c, flat(wc.at[1]), c)
     keep_right(1, panel_c[1], cor_c[1])
@@ -787,14 +785,14 @@
         ((2, rows, 2 * NB), bf16),
         ((2, 2 * NB, rows), bf16),
         ((2, 2 * NB, rows), bf16),
-        ((5, 3, NB, NB), f32),
-        ((5, n, 3, pc, NB), f32),
-        ((5, 6, NB, NB), f32),
-        ((2, NB, NB), f32),
-        ((2, n, pc, NB), f32),
-        ((2, pc, NB), f32),
-        ((2, n, pc, NB), f32),
-        ((2, NB, NB), f32),
+        ((4, 3, NB, NB), f32),
+        ((4, n, 3, pc, NB), f32),
+        ((4, 6, NB, NB), f32),
+        ((4, NB, NB), f32),
+        ((4, n, pc, NB), f32),
+        ((4, pc, NB), f32),
+        ((4, n, pc, NB), f32),
+        ((4, NB, NB), f32),
     ] + [((NB, NB), f32)] * 5
     anywhere = pl.BlockSpec(memory_space=pl.ANY)
     left = jax.ShapeDtypeStruct((rows, 2 * NB), bf16)
@@ -806,7 +804,7 @@
         out_specs=[anywhere] * 5,
         scratch_shapes=[pltpu.VMEM(*shape) for shape in shapes]
         + [pltpu.SemaphoreType.DMA] * 5
-        + [pltpu.SemaphoreType.DMA((51,))] * 2,
+        + [pltpu.SemaphoreType.DMA((55,))] * 2,
         compiler_params=pltpu.CompilerParams(
             collective_id=0, has_side_effects=True, vmem_limit_bytes=VMEM_LIMIT
         ),

time: 118 us -> 111 us (0.941)
  Pallas kernels: 117 us -> 110 us
    pallas_call x1, Pallas kernels: 111 us -> 104 us  [local(): pl.pallas_call(functools.partial(reduce_kernel, n, tiles), out_shape=[jax...]
where the time goes in v6:
time: 111 us; the launch traced here: 110 us
  Pallas kernels  110 us (99%)
    pallas_call x1, Pallas kernels, local(): pl.pallas_call(functools.partial(reduce_kernel, n, tiles), out_shape=[jax...  104 us
    pallas_call x1, Pallas kernels, local(): pl.pallas_call(functools.partial(update_kernel, tiles), out_shape=jax.Sha...  6.67 us

profile of v6, /device:TPU:1, one launch (start us, length us, event | category | flops | bytes accessed | tf_op | source)
XLA Modules:
  0.0 110.4 jit_solution(8256928198170038401)
XLA Ops:
  0.0 103.7 %reduce_panels.1 = (f32[8192,128]{1,0:T(8,128)}, bf16[1024,256]{1,0:T(8,128)(2,1)}, bf16[1024,256]{1,0:T(8,128)(2,1)}, bf16[256,1024]{1,0:T(8,128)(2,1)}, bf16[256,1024]{1,0:T(8,128)(2,1)}) custom-call(f32[8192,128]{1,0:T(8,128)} %bitcast.4), custom_call_target="tpu_custom_call" | custom-call | tf_op jit(solution)/shard_map/reduce_panels/pallas_call | solution.py:800
  103.7 6.7 %update_matrix.1 = f32[8192,128]{1,0:T(8,128)} custom-call(f32[8192,128]{1,0:T(8,128)} %get-tuple-element.10.a_ref, bf16[1024,256]{1,0:T(8,128)(2,1)} %get-tuple-element.11.lh, bf16[1024,256]{1,0:T(8,128)(2,1)} %get-tuple-element.12.ll, bf16[256,1024]{1,0:T(8,128)(2,1)} %get-tuple-element.13.qh, bf16[256,1024]{1,0:T(8,128)(2,1)} %get-tuple-element.14.ql), custom_call_target="tpu_custom_call" | custom-call | tf_op jit(solution)/shard_map/update_matrix/pallas_call | solution.py:817

commit v7 on v6

--- a/solution.py
+++ b/solution.py
@@ -541,12 +541,6 @@
     gather_rows_mid(xc.at[1], 11)
     all_mid(2, 49, over_rows, r)
 
-    @pl.when(r != c)
-    def _():
-        wait_received(22, wc.at[0, level, parity])
-        wait_sent(22, wch.at[0])
-
-    gather_rows_start(wc.at[0], 24)
     wait(48, ar_res.at[0, pl.ds(3, 3), pl.ds(0, (n - 1) * pc)])
     sum_wait(1, 1, 14)
     r0 = r0_ref[...]
@@ -594,12 +588,20 @@
         def _():
             f_ref[1, 0:NB, :] = zero_tile
 
+    all_late(2, 49, over_cols, c)
     first_panel(panel_r, cor_r, xr[0], xr[1], r)
     gather_cols_wait(wr.at[0], 23)
     first_panel_product(panel_r, cor_r, wr[0], r)
 
     p1r = panel_r[1]
     sum_start(2, [dot3(p1r, p1r, TN)], 30, over_rows, r)
+
+    @pl.when(r != c)
+    def _():
+        wait_received(22, wc.at[0, level, parity])
+        wait_sent(22, wch.at[0])
+
+    gather_rows_start(wc.at[0], 24)
     both = halves(p1r)
 
     def second_product(b, carry):
@@ -612,7 +614,6 @@
 
     lax.fori_loop(0, tiles, second_product, 0)
     send(wpart_c.at[:, 1 - parity], wsib, 34, sibling)
-    all_late(2, 49, over_cols, c)
     sum_mid(2, 1, 30, over_rows, r)
     wait(34, wsib)
     wsum[...] = wpart_c[:, parity] + wsib[...]
@@ -624,6 +625,11 @@
 
     lax.fori_loop(1, half, spread, 0)
     wslot_c[level] = wsum[level]
+    all_wait(2, 49)
+    c02 = exact(h_res[2], z0) + exact(x12, rz0) - exact(f02, b0)
+    top = x12 - exact(c02, f01, NT) - exact(f02, c01, NT)
+    cf = exact(c02, f02, NT)
+    keep_left(0, cor_r[0], panel_r[0])
     gather_rows_mid(wc.at[0], 24)
     all_start(3, dot3(xr[2, pl.ds(c * ch, ch), :], panel_r[1, pl.ds(c * ch, ch), :], TN), 52, over_cols, c)
     gather_rows_wait(xc.at[1], 11)
@@ -634,8 +640,6 @@
     all_start(1, dot3(p1c, flat(wpart_c), TN), 36, over_cols, c)
     inner = dot3(p1c, jnp.concatenate([panel_c[0], cor_c[0]], axis=1), TN)
     sum_start(3, [inner[:, 0:NB], inner[:, NB:]], 32, over_cols, c)
-    keep_left(0, cor_r[0], panel_r[0])
-    keep_right(0, panel_c[0], cor_c[0])
     sum_wait(2, 1, 30)
     g_ref[...] = ar_res[2, 0]
     cholesky_blocks(g_ref, r1_ref, 0, CHOL_BLOCKS)
@@ -659,9 +663,6 @@
 
     wc[1, level, parity] = total
     gather_rows_start(wc.at[1], 39)
-    all_wait(2, 49)
-    c02 = exact(h_res[2], z0) + exact(x12, rz0) - exact(f02, b0)
-    top = x12 - exact(c02, f01, NT) - exact(f02, c01, NT)
     y_ref[...] = ar_res[2, 0] + exact(top, r1_ref[...], TN)
     inverse_blocks(y_ref, t_ref, 0, INV_BLOCKS // 2)
 
@@ -683,11 +684,11 @@
     j1t = ar_res[3, 0]
     j2t = ar_res[3, 1]
     cross = exact(j2t, j1t, NT)
-    cf = exact(c02, f02, NT)
     k1 = h_res[3].T - exact(j2t, f02, NT) - exact(j1t, c02, NT)
     known = known_part(r1, k1, x22 - cf - cf.T) - cross - cross.T
     fold1 = -exact(j1t, z1, TN) - exact(f02, rz1, TN)
     fold2 = -exact(j2t, z1, TN) - exact(c02, rz1, TN)
+    keep_right(0, panel_c[0], cor_c[0])
     apply_first()
     write_band(0, r0_ref)
     write_band(1, r1_ref)

time: 111 us -> 114 us (1.027); the launches traced: 110 us -> 112 us
  Pallas kernels: 110 us -> 112 us
    pallas_call x1, Pallas kernels: 104 us -> 105 us  [local(): pl.pallas_call(functools.partial(reduce_kernel, n, tiles), out_shape=[jax...]
where the time goes in v7:
time: 114 us; the launch traced here: 112 us
  Pallas kernels  112 us (98%)
    pallas_call x1, Pallas kernels, local(): pl.pallas_call(functools.partial(reduce_kernel, n, tiles), out_shape=[jax...  105 us
    pallas_call x1, Pallas kernels, local(): pl.pallas_call(functools.partial(update_kernel, tiles), out_shape=jax.Sha...  6.67 us

profile of v7, /device:TPU:1, one launch (start us, length us, event | category | flops | bytes accessed | tf_op | source)
XLA Modules:
  0.0 112.1 jit_solution(2823507124750284004)
XLA Ops:
  0.0 105.4 %reduce_panels.1 = (f32[8192,128]{1,0:T(8,128)}, bf16[1024,256]{1,0:T(8,128)(2,1)}, bf16[1024,256]{1,0:T(8,128)(2,1)}, bf16[256,1024]{1,0:T(8,128)(2,1)}, bf16[256,1024]{1,0:T(8,128)(2,1)}) custom-call(f32[8192,128]{1,0:T(8,128)} %bitcast.4), custom_call_target="tpu_custom_call" | custom-call | tf_op jit(solution)/shard_map/reduce_panels/pallas_call | solution.py:801
  105.4 6.7 %update_matrix.1 = f32[8192,128]{1,0:T(8,128)} custom-call(f32[8192,128]{1,0:T(8,128)} %get-tuple-element.10.a_ref, bf16[1024,256]{1,0:T(8,128)(2,1)} %get-tuple-element.11.lh, bf16[1024,256]{1,0:T(8,128)(2,1)} %get-tuple-element.12.ll, bf16[256,1024]{1,0:T(8,128)(2,1)} %get-tuple-element.13.qh, bf16[256,1024]{1,0:T(8,128)(2,1)} %get-tuple-element.14.ql), custom_call_target="tpu_custom_call" | custom-call | tf_op jit(solution)/shard_map/update_matrix/pallas_call | solution.py:818

commit v8 on v7

--- a/solution.py
+++ b/solution.py
@@ -519,7 +519,6 @@
     for j in range(1, n):
         total = total + wslot_r[j]
     wr[0, pl.ds(c * ch, ch), :] = total
-    gather_cols_start(wr.at[0], 23)
     wch[0] = total
 
     @pl.when(r != c)
@@ -530,6 +529,7 @@
     def _():
         wc[0, level, parity] = total
 
+    gather_cols_start(wr.at[0], 23)
     all_late(0, 26, over_rows, r)
     sum_mid(1, 1, 14, over_rows, r)
     row_wait(46, 1, 3, 2)
@@ -541,6 +541,12 @@
     gather_rows_mid(xc.at[1], 11)
     all_mid(2, 49, over_rows, r)
 
+    @pl.when(r != c)
+    def _():
+        wait_received(22, wc.at[0, level, parity])
+        wait_sent(22, wch.at[0])
+
+    gather_rows_start(wc.at[0], 24)
     wait(48, ar_res.at[0, pl.ds(3, 3), pl.ds(0, (n - 1) * pc)])
     sum_wait(1, 1, 14)
     r0 = r0_ref[...]
@@ -595,13 +601,6 @@
 
     p1r = panel_r[1]
     sum_start(2, [dot3(p1r, p1r, TN)], 30, over_rows, r)
-
-    @pl.when(r != c)
-    def _():
-        wait_received(22, wc.at[0, level, parity])
-        wait_sent(22, wch.at[0])
-
-    gather_rows_start(wc.at[0], 24)
     both = halves(p1r)
 
     def second_product(b, carry):

time: 114 us -> 111 us (0.974)
  Pallas kernels: 112 us -> 109 us
    pallas_call x1, Pallas kernels: 105 us -> 102 us  [local(): pl.pallas_call(functools.partial(reduce_kernel, n, tiles), out_shape=[jax...]
where the time goes in v8:
time: 111 us; the launch traced here: 109 us
  Pallas kernels  109 us (98%)
    pallas_call x1, Pallas kernels, local(): pl.pallas_call(functools.partial(reduce_kernel, n, tiles), out_shape=[jax...  102 us
    pallas_call x1, Pallas kernels, local(): pl.pallas_call(functools.partial(update_kernel, tiles), out_shape=jax.Sha...  6.67 us

profile of v8, /device:TPU:1, one launch (start us, length us, event | category | flops | bytes accessed | tf_op | source)
XLA Modules:
  0.0 109.0 jit_solution(887625211525196813)
XLA Ops:
  0.0 102.4 %reduce_panels.1 = (f32[8192,128]{1,0:T(8,128)}, bf16[1024,256]{1,0:T(8,128)(2,1)}, bf16[1024,256]{1,0:T(8,128)(2,1)}, bf16[256,1024]{1,0:T(8,128)(2,1)}, bf16[256,1024]{1,0:T(8,128)(2,1)}) custom-call(f32[8192,128]{1,0:T(8,128)} %bitcast.4), custom_call_target="tpu_custom_call" | custom-call | tf_op jit(solution)/shard_map/reduce_panels/pallas_call | solution.py:800
  102.4 6.7 %update_matrix.1 = f32[8192,128]{1,0:T(8,128)} custom-call(f32[8192,128]{1,0:T(8,128)} %get-tuple-element.10.a_ref, bf16[1024,256]{1,0:T(8,128)(2,1)} %get-tuple-element.11.lh, bf16[1024,256]{1,0:T(8,128)(2,1)} %get-tuple-element.12.ll, bf16[256,1024]{1,0:T(8,128)(2,1)} %get-tuple-element.13.qh, bf16[256,1024]{1,0:T(8,128)(2,1)} %get-tuple-element.14.ql), custom_call_target="tpu_custom_call" | custom-call | tf_op jit(solution)/shard_map/update_matrix/pallas_call | solution.py:817
